TPU v7x, 128 devices: a whole 4x4x4 slice. The times are simulated.
128 devices in a mesh: gy: 8 (over z_hi, y), gx: 16 (over x, z_lo, core).
Axes of the slice: x: 4, y: 4, z: 4 (z_hi: 2, z_lo: 2; z = z_hi * 2 + z_lo), core: 2. Of those that a mesh axis runs over, the one named last changes fastest.
Arguments:
- obj: float32 [2, 2048, 4096], P(None, 'gy', 'gx'), may hold values from -5 to 5
- probe: float32 [2, 256, 256], replicated, may hold values from -6 to 6
- positions: int32 [8, 16, 8, 2], P('gy', 'gx'), may hold values from -128 to 3967, as said below
- amps: bfloat16 [8, 16, 8, 256, 256], P('gy', 'gx'), may hold values from 0 to 2
Outputs:
- obj_new: float32 [2, 2048, 4096], P(None, 'gy', 'gx')
- probe_new: float32 [2, 256, 256], replicated
Inputs may be any that keep to these rules, and one draw needn't show every extreme that they name: `positions`: for the entry at [ty, tx, k], both coordinates plus 128 lie in the tile, that is row within [ty * 256, (ty + 1) * 256) and column within [tx * 256, (tx + 1) * 256).
All inputs are finite; a program needn't handle non-finite values.
Results may differ from a plain program's by a relative error of at most 0.0003.
Values sent between devices are 32-bit elements; how exact they have to be, the bound alone decides.
A program may use at most 128 MiB of HBM per device.

v0:
```python
import math

import jax
import jax.numpy as jnp
from jax import lax
from jax.sharding import PartitionSpec as P

ITERS = 2


def with_halo(cells, sides, width):
    for axis, dim in sides:
        count = lax.axis_size(axis)
        ends = count - 1
        head = lax.slice_in_dim(cells, 0, width, axis=dim)
        tail = lax.slice_in_dim(cells, cells.shape[dim] - width, cells.shape[dim], axis=dim)
        cells = jnp.concatenate(
            [
                lax.ppermute(tail, axis, [(i, (i + 1) % count) for i in range(ends)]),
                cells,
                lax.ppermute(head, axis, [((i + 1) % count, i) for i in range(ends)]),
            ],
            axis=dim,
        )
    return cells


def dft_tables(size, sign):
    index = jnp.arange(size, dtype=jnp.int32)
    turns = index[:, None] * index[None, :] % size
    angle = turns.astype(jnp.float32) * (2.0 * math.pi / size)
    scale = 1.0 / math.sqrt(size)
    real_part = jnp.cos(angle) * scale
    imag_part = sign * jnp.sin(angle) * scale
    left = jnp.stack([jnp.stack([real_part, -imag_part]), jnp.stack([imag_part, real_part])])
    right = jnp.stack([jnp.stack([real_part, imag_part]), jnp.stack([-imag_part, real_part])])
    return (left, right)


def transform(field, tables):
    left, right = tables
    middle = jnp.einsum("abjk,pbkl->pajl", left, field, precision=lax.Precision.HIGHEST)
    return jnp.einsum("pbjk,bakl->pajl", middle, right, precision=lax.Precision.HIGHEST)


def shards(obj, probe, positions, amps):
    tile = obj.shape[1]
    patch = probe.shape[1]
    half = patch // 2
    count = positions.shape[2]
    forward = dft_tables(patch, -1.0)
    backward = dft_tables(patch, 1.0)
    anchor = jnp.stack([lax.axis_index("gy") * tile, lax.axis_index("gx") * tile])
    local = positions.reshape(count, 2) - anchor[None, :] + half
    measured = amps.reshape(count, patch, patch).astype(jnp.float32)
    extent = tile + patch
    for step in range(ITERS):
        extended = with_halo(obj, (("gy", 1), ("gx", 2)), half)
        patches = jax.vmap(
            lambda corner: lax.dynamic_slice(extended, (0, corner[0], corner[1]), (2, patch, patch))
        )(local)
        probe_re = probe[0]
        probe_im = probe[1]
        obj_re = patches[:, 0]
        obj_im = patches[:, 1]
        exit_wave = jnp.stack(
            [probe_re * obj_re - probe_im * obj_im, probe_re * obj_im + probe_im * obj_re], axis=1
        )
        far = transform(exit_wave, forward)
        magnitude = jnp.maximum(jnp.sqrt(far[:, 0] * far[:, 0] + far[:, 1] * far[:, 1]), 0.5)
        factor = measured / magnitude - 1.0
        chi = transform(far * factor[:, None], backward)
        chi_re = chi[:, 0]
        chi_im = chi[:, 1]
        grads = jnp.stack(
            [probe_re * chi_re + probe_im * chi_im, probe_re * chi_im - probe_im * chi_re], axis=1
        )
        grad_probe = jnp.stack(
            [
                jnp.sum(obj_re * chi_re + obj_im * chi_im, axis=0),
                jnp.sum(obj_re * chi_im - obj_im * chi_re, axis=0),
            ]
        )
        weight = jnp.sum(obj_re * obj_re + obj_im * obj_im, axis=0)
        peak = jnp.max(probe_re * probe_re + probe_im * probe_im)

        def deposit(item, total):
            corner = local[item]
            current = lax.dynamic_slice(total, (0, corner[0], corner[1]), (2, patch, patch))
            return lax.dynamic_update_slice(total, current + grads[item], (0, corner[0], corner[1]))

        grad_ext = lax.fori_loop(0, count, deposit, jnp.zeros((2, extent, extent), jnp.float32))
        framed = with_halo(grad_ext, (("gy", 1), ("gx", 2)), half)
        inner = slice(2 * half, 2 * half + tile)
        low = slice(0, half)
        high = slice(extent + half, extent + 2 * half)
        tile_grad = grad_ext[:, half : half + tile, half : half + tile]
        tile_grad = tile_grad.at[:, :half, :].add(framed[:, low, inner])
        tile_grad = tile_grad.at[:, tile - half :, :].add(framed[:, high, inner])
        tile_grad = tile_grad.at[:, :, :half].add(framed[:, inner, low])
        tile_grad = tile_grad.at[:, :, tile - half :].add(framed[:, inner, high])
        tile_grad = tile_grad.at[:, :half, :half].add(framed[:, low, low])
        tile_grad = tile_grad.at[:, :half, tile - half :].add(framed[:, low, high])
        tile_grad = tile_grad.at[:, tile - half :, :half].add(framed[:, high, low])
        tile_grad = tile_grad.at[:, tile - half :, tile - half :].add(framed[:, high, high])
        new_obj = obj + tile_grad / peak
        total_grad, total_weight = lax.psum((grad_probe, weight), ("gy", "gx"))
        probe = probe + total_grad / (0.9 * total_weight + 0.1 * jnp.max(total_weight))[None]
        obj = new_obj
    return (obj, probe)


def solution(mesh):
    in_specs = (
        P(None, "gy", "gx"),
        P(),
        P("gy", "gx", None, None),
        P("gy", "gx", None, None, None),
    )
    out_specs = (P(None, "gy", "gx"), P())
    return jax.shard_map(shards, mesh=mesh, in_specs=in_specs, out_specs=out_specs, check_vma=False)
```

profile of v0, /device:TPU:1, one launch (start us, length us, event | category | flops | bytes accessed | tf_op | source)
XLA Modules:
  0.0 820.1 jit_solution(10316529358436779313)
XLA Ops:
  8.3 4.0 collective-permute-start
  17.4 3.7 collective-permute-done.1
  22.3 5.3 collective-permute-start.2
  27.6 1.9 collective-permute-start.3
  33.9 2.1 fusion.44
  36.0 3.6 collective-permute-done.2
  41.0 2.4 broadcast.494.clone2
  43.4 26.3 %while.46 = (s32[]{:T(128)}, f32[2,512,512]{2,1,0:T(8,128)S(1)}, s32[8,3]{0,1:T(4,128)S(1)}, f32[8,2,256,256]{2,3,0,1:T(8,128)}, s32[]{:T(128)}) while((s32[]{:T(128)}, f32[2,512,512]{2,1,0:T(8,128)S(1)}, s32[8,3]{0,1:T(4,128)S(1)}, f32[8,2,256,256]{2,3,0,1:T(8,128)}, s32[]{:T(128)}) %tuple.194), condition=%wide.while_cond.16, body=%wide.while_body.16.sunk | while | flops 2 | bytes 3146353 | solution.py:60
  69.8 2.9 multiply_subtract_fusion.3
  72.7 7.5 fusion.14
  80.3 7.6 fusion.16
  89.1 7.6 fusion.12
  96.7 7.3 fusion.19
  104.1 2.3 add_reduce_fusion.3
  106.4 2.3 pad_maximum_fusion
  108.9 118.3 %while.44 = (s32[]{:T(128)}, f32[2,512,512]{2,1,0:T(8,128)S(1)}, s32[8,2]{0,1:T(2,128)S(1)}, f32[8,2,256,256]{2,3,0,1:T(8,128)}, s32[]{:T(128)}, /*index=5*/s32[]{:T(128)}, s32[]{:T(128)}) while((s32[]{:T(128)}, f32[2,512,512]{2,1,0:T(8,128)S(1)}, s32[8,2]{0,1:T(2,128)S(1)}, f32[8,2,256,256]{2,3,0,1:T(8,128)}, s32[]{:T(128)}, ...), condition=%wide.region_1.2_spmd, body=%wide.region_0.1_spmd.sunk | while | flops 131080 | bytes 4718789 | solution.py:92
  114.9 10.8 %dynamic_update_slice.16 = f32[2,512,512]{2,1,0:T(8,128)S(1)} dynamic-update-slice(f32[2,512,512]{2,1,0:T(8,128)S(1)} %get-tuple-element.631, f32[2,256,256]{2,1,0:T(8,128)S(1)} %bitcast_add_fusion.4, s32[]{:T(128)} %constant.475.clone.1..sunk, s32[]{:T(128)S(6)} %select_n.142, s32[]{:T(128)S(6)} %select_n.143) | dynamic-update-slice | bytes 1048580 | tf_op jit(solution)/shard_map/while/body/eval_jaxpr/dynamic_update_slice | solution.py:90
  131.6 7.5 dynamic_update_slice.16
  145.1 9.8 %dynamic_update_slice.16 = f32[2,512,512]{2,1,0:T(8,128)S(1)} dynamic-update-slice(f32[2,512,512]{2,1,0:T(8,128)S(1)} %get-tuple-element.631, f32[2,256,256]{2,1,0:T(8,128)S(1)} %bitcast_add_fusion.4, s32[]{:T(128)} %constant.475.clone.1..sunk, s32[]{:T(128)S(6)} %select_n.142, s32[]{:T(128)S(6)} %select_n.143) | dynamic-update-slice | bytes 1048580 | tf_op jit(solution)/shard_map/while/body/eval_jaxpr/dynamic_update_slice | solution.py:90
  161.0 7.8 dynamic_update_slice.16
  174.8 10.6 %dynamic_update_slice.16 = f32[2,512,512]{2,1,0:T(8,128)S(1)} dynamic-update-slice(f32[2,512,512]{2,1,0:T(8,128)S(1)} %get-tuple-element.631, f32[2,256,256]{2,1,0:T(8,128)S(1)} %bitcast_add_fusion.4, s32[]{:T(128)} %constant.475.clone.1..sunk, s32[]{:T(128)S(6)} %select_n.142, s32[]{:T(128)S(6)} %select_n.143) | dynamic-update-slice | bytes 1048580 | tf_op jit(solution)/shard_map/while/body/eval_jaxpr/dynamic_update_slice | solution.py:90
  191.4 8.8 %dynamic_update_slice.16 = f32[2,512,512]{2,1,0:T(8,128)S(1)} dynamic-update-slice(f32[2,512,512]{2,1,0:T(8,128)S(1)} %get-tuple-element.631, f32[2,256,256]{2,1,0:T(8,128)S(1)} %bitcast_add_fusion.4, s32[]{:T(128)} %constant.475.clone.1..sunk, s32[]{:T(128)S(6)} %select_n.142, s32[]{:T(128)S(6)} %select_n.143) | dynamic-update-slice | bytes 1048580 | tf_op jit(solution)/shard_map/while/body/eval_jaxpr/dynamic_update_slice | solution.py:90
  206.2 8.0 dynamic_update_slice.16
  220.1 7.1 dynamic_update_slice.16
  227.3 1.7 collective-permute-start.4
  231.0 9.2 %collective-permute-done.4 = f32[2,128,512]{2,1,0:T(8,128)S(1)} collective-permute-done((f32[2,128,512]{2,1,0:T(8,128)S(1)}, f32[2,128,512]{2,1,0:T(8,128)S(1)}, u32[]{:S(2)}, u32[]{:S(2)}) %collective-permute-start.4) | collective-permute-done | bytes 524320 | tf_op jit(solution)/shard_map/ppermute | solution.py:19
  241.2 3.1 collective-permute-done.5
  245.6 8.8 %collective-permute-start.6 = (f32[2,768,128]{2,1,0:T(8,128)}, f32[2,768,128]{2,1,0:T(8,128)}, u32[]{:S(2)}, u32[]{:S(2)}) collective-permute-start(f32[2,768,128]{2,1,0:T(8,128)} %get-tuple-element.453), channel_id=1, source_target_pairs={{0,1},{1,2},{2,3},{3,4},{4,5},{5,6},{6,7},{7,8},{8,9},{9,10},{10,1... | collective-permute-start | bytes 2359304 | tf_op jit(solution)/shard_map/ppermute | solution.py:19
  255.7 1.9 collective-permute-start.7
  260.6 11.5 %collective-permute-done.6 = f32[2,768,128]{2,1,0:T(8,128)} collective-permute-done((f32[2,768,128]{2,1,0:T(8,128)}, f32[2,768,128]{2,1,0:T(8,128)}, u32[]{:S(2)}, u32[]{:S(2)}) %collective-permute-start.6) | collective-permute-done | bytes 786464 | tf_op jit(solution)/shard_map/ppermute | solution.py:19
  275.1 2.8 add_select_fusion.2
  277.8 2.4 scatter-add.61
  282.8 6.4 collective-permute-start.8
  290.7 123.6 %all-reduce.7.cloned.1.call-done = (f32[2,256,256]{1,2,0:T(8,128)}, f32[256,256]{0,1:T(8,128)}) async-done(((f32[2,256,256]{1,2,0:T(8,128)}, f32[256,256]{0,1:T(8,128)}), (f32[2,256,256]{1,2,0:T(8,128)}, f32[256,256]{0,1:T(8,128)})) %all-reduce.7.cloned.1.call-update) | async-done | bytes 786448 | tf_op jit(solution)/shard_map/psum | solution.py:107
  414.3 1.6 reduce_max.37
  417.4 3.4 collective-permute-start.10
  420.8 1.9 collective-permute-start.11
  423.7 8.8 %collective-permute-done.10 = f32[2,512,128]{2,1,0:T(8,128)S(1)} collective-permute-done((f32[2,512,128]{2,1,0:T(8,128)S(1)}, f32[2,512,128]{2,1,0:T(8,128)S(1)}, u32[]{:S(2)}, u32[]{:S(2)}) %collective-permute-start.10) | collective-permute-done | bytes 524320 | tf_op jit(solution)/shard_map/ppermute | solution.py:19
  432.8 2.4 broadcast.494.clone
  435.2 25.0 %while.47 = (s32[]{:T(128)}, f32[2,512,512]{2,1,0:T(8,128)S(1)}, s32[8,3]{0,1:T(4,128)S(1)}, f32[8,2,256,256]{2,3,0,1:T(8,128)}, s32[]{:T(128)}) while((s32[]{:T(128)}, f32[2,512,512]{2,1,0:T(8,128)S(1)}, s32[8,3]{0,1:T(4,128)S(1)}, f32[8,2,256,256]{2,3,0,1:T(8,128)}, s32[]{:T(128)}) %tuple.212), condition=%wide.while_cond.17, body=%wide.while_body.17.sunk | while | flops 2 | bytes 3146353 | solution.py:60
  460.3 2.9 multiply_subtract_fusion.1
  463.2 7.5 fusion.10
  470.7 7.4 fusion.22
  479.3 7.6 fusion.8
  487.0 7.4 fusion.25
  494.4 2.3 add_reduce_fusion.1
  496.7 2.3 pad_maximum_fusion.1
  499.2 118.6 %while.45 = (s32[]{:T(128)}, f32[2,512,512]{2,1,0:T(8,128)S(1)}, s32[8,2]{0,1:T(2,128)S(1)}, f32[8,2,256,256]{2,3,0,1:T(8,128)}, s32[]{:T(128)}, /*index=5*/s32[]{:T(128)}, s32[]{:T(128)}) while((s32[]{:T(128)}, f32[2,512,512]{2,1,0:T(8,128)S(1)}, s32[8,2]{0,1:T(2,128)S(1)}, f32[8,2,256,256]{2,3,0,1:T(8,128)}, s32[]{:T(128)}, ...), condition=%wide.region_11.12_spmd, body=%wide.region_10.11_spmd.sunk | while | flops 131080 | bytes 4718789 | solution.py:92
  505.3 10.8 %dynamic_update_slice.17 = f32[2,512,512]{2,1,0:T(8,128)S(1)} dynamic-update-slice(f32[2,512,512]{2,1,0:T(8,128)S(1)} %get-tuple-element.667, f32[2,256,256]{2,1,0:T(8,128)S(1)} %bitcast_add_fusion.5, s32[]{:T(128)} %constant.475.clone.1..sunk.1, s32[]{:T(128)S(6)} %select_n.144, s32[]{:T(128)S(6)} %select_n.145) | dynamic-update-slice | bytes 1048580 | tf_op jit(solution)/shard_map/while/body/eval_jaxpr/dynamic_update_slice | solution.py:90
  522.0 7.5 dynamic_update_slice.17
  535.6 9.8 %dynamic_update_slice.17 = f32[2,512,512]{2,1,0:T(8,128)S(1)} dynamic-update-slice(f32[2,512,512]{2,1,0:T(8,128)S(1)} %get-tuple-element.667, f32[2,256,256]{2,1,0:T(8,128)S(1)} %bitcast_add_fusion.5, s32[]{:T(128)} %constant.475.clone.1..sunk.1, s32[]{:T(128)S(6)} %select_n.144, s32[]{:T(128)S(6)} %select_n.145) | dynamic-update-slice | bytes 1048580 | tf_op jit(solution)/shard_map/while/body/eval_jaxpr/dynamic_update_slice | solution.py:90
  551.4 7.8 dynamic_update_slice.17
  565.3 10.6 %dynamic_update_slice.17 = f32[2,512,512]{2,1,0:T(8,128)S(1)} dynamic-update-slice(f32[2,512,512]{2,1,0:T(8,128)S(1)} %get-tuple-element.667, f32[2,256,256]{2,1,0:T(8,128)S(1)} %bitcast_add_fusion.5, s32[]{:T(128)} %constant.475.clone.1..sunk.1, s32[]{:T(128)S(6)} %select_n.144, s32[]{:T(128)S(6)} %select_n.145) | dynamic-update-slice | bytes 1048580 | tf_op jit(solution)/shard_map/while/body/eval_jaxpr/dynamic_update_slice | solution.py:90
  581.9 8.8 %dynamic_update_slice.17 = f32[2,512,512]{2,1,0:T(8,128)S(1)} dynamic-update-slice(f32[2,512,512]{2,1,0:T(8,128)S(1)} %get-tuple-element.667, f32[2,256,256]{2,1,0:T(8,128)S(1)} %bitcast_add_fusion.5, s32[]{:T(128)} %constant.475.clone.1..sunk.1, s32[]{:T(128)S(6)} %select_n.144, s32[]{:T(128)S(6)} %select_n.145) | dynamic-update-slice | bytes 1048580 | tf_op jit(solution)/shard_map/while/body/eval_jaxpr/dynamic_update_slice | solution.py:90
  596.7 8.0 dynamic_update_slice.17
  610.7 7.1 dynamic_update_slice.17
  618.9 2.1 collective-permute-start.12
  624.0 150.8 %all-reduce.5.cloned.1.call-done = (f32[2,256,256]{1,2,0:T(8,128)}, f32[256,256]{0,1:T(8,128)}) async-done(((f32[2,256,256]{1,2,0:T(8,128)}, f32[256,256]{0,1:T(8,128)}), (f32[2,256,256]{1,2,0:T(8,128)}, f32[256,256]{0,1:T(8,128)})) %all-reduce.5.cloned.1.call-update) | async-done | bytes 786448 | tf_op jit(solution)/shard_map/psum | solution.py:107
  780.6 3.2 collective-permute-start.14
  783.9 2.0 collective-permute-start.15
  786.8 2.0 copy.33
  790.9 10.6 %collective-permute-done.14 = f32[2,768,128]{2,1,0:T(8,128)} collective-permute-done((f32[2,768,128]{2,1,0:T(8,128)}, f32[2,768,128]{2,1,0:T(8,128)}, u32[]{:S(2)}, u32[]{:S(2)}) %collective-permute-start.14) | collective-permute-done | bytes 786464 | tf_op jit(solution)/shard_map/ppermute | solution.py:19
  804.5 2.8 add_select_fusion.1
  807.2 2.4 scatter-add.75
  (337 shorter events, 136.4 us)
Async XLA Ops:
  7.2 10.2 %copy-start.8 = (f32[2,256,256]{2,1,0:T(8,128)S(1)}, f32[2,256,256]{2,1,0:T(8,128)}, u32[]{:S(2)}) copy-start(f32[2,256,256]{2,1,0:T(8,128)} %param.40) | copy-start | bytes 1572868
  7.2 7.7 copy-start.44
  7.2 407.2 %all-reduce.7.cloned.1.call-start = ((), (), s32[]{:S(2)}) async-start(), calls=%async_computation.1 | async-start | bytes 1572864 | tf_op jit(solution)/shard_map/psum | solution.py:107
  8.3 9.0 %collective-permute-start = (f32[2,128,256]{2,1,0:T(8,128)S(1)}, f32[2,128,256]{2,1,0:T(8,128)S(1)}, u32[]{:S(2)}, u32[]{:S(2)}) collective-permute-start(f32[2,128,256]{2,1,0:T(8,128)S(1)} %get-tuple-element.477), channel_id=1, source_target_pairs={{0,16},{16,32},{32,48},{48,64},{64,80},{80,96},{96,112},{1,17},{17... | collective-permute-start | bytes 786440 | tf_op jit(solution)/shard_map/ppermute | solution.py:19
  12.4 8.8 %collective-permute-start.1 = (f32[2,128,256]{2,1,0:T(8,128)S(1)}, f32[2,128,256]{2,1,0:T(8,128)S(1)}, u32[]{:S(2)}, u32[]{:S(2)}) collective-permute-start(f32[2,128,256]{2,1,0:T(8,128)S(1)} %get-tuple-element.476), channel_id=1, source_target_pairs={{16,0},{32,16},{48,32},{64,48},{80,64},{96,80},{112,96},{17,1},{33... | collective-permute-start | bytes 786440 | tf_op jit(solution)/shard_map/ppermute | solution.py:21
  17.4 13.1 %copy-start.33 = (bf16[1,1,8,256,256]{4,3,2,1,0:T(8,128)(2,1)S(1)}, bf16[1,1,8,256,256]{4,3,2,1,0:T(8,128)(2,1)}, u32[]{:S(2)}) copy-start(bf16[1,1,8,256,256]{4,3,2,1,0:T(8,128)(2,1)} %param.43) | copy-start | bytes 3145732
  22.3 17.3 %collective-permute-start.2 = (f32[2,512,128]{2,1,0:T(8,128)}, f32[2,512,128]{2,1,0:T(8,128)}, u32[]{:S(2)}, u32[]{:S(2)}) collective-permute-start(f32[2,512,128]{2,1,0:T(8,128)} %get-tuple-element.460), channel_id=1, source_target_pairs={{0,1},{1,2},{2,3},{3,4},{4,5},{5,6},{6,7},{7,8},{8,9},{9,10},{10,1... | collective-permute-start | bytes 1572872 | tf_op jit(solution)/shard_map/ppermute | solution.py:19
  27.6 12.0 %collective-permute-start.3 = (f32[2,512,128]{2,1,0:T(8,128)}, f32[2,512,128]{2,1,0:T(8,128)}, u32[]{:S(2)}, u32[]{:S(2)}) collective-permute-start(f32[2,512,128]{2,1,0:T(8,128)} %get-tuple-element.461), channel_id=1, source_target_pairs={{1,0},{2,1},{3,2},{4,3},{5,4},{6,5},{7,6},{8,7},{9,8},{10,9},{11,1... | collective-permute-start | bytes 1572872 | tf_op jit(solution)/shard_map/ppermute | solution.py:21
  69.7 2.9 copy-start.23
  69.8 2.9 copy-start.25
  72.7 7.6 copy-start.19
  72.7 7.6 copy-start.21
  80.2 7.6 copy-start.4
  87.9 1.1 copy-start.15
  87.9 1.2 copy-start.17
  89.1 7.6 copy-start.11
  89.1 7.6 copy-start.13
  96.7 7.4 copy-start
  96.7 7.4 copy-start.27
  227.2 3.1 copy-start.45
  227.3 12.8 %collective-permute-start.4 = (f32[2,128,512]{2,1,0:T(8,128)S(1)}, f32[2,128,512]{2,1,0:T(8,128)S(1)}, u32[]{:S(2)}, u32[]{:S(2)}) collective-permute-start(f32[2,128,512]{2,1,0:T(8,128)S(1)} %get-tuple-element.457), channel_id=1, source_target_pairs={{0,16},{16,32},{32,48},{48,64},{64,80},{80,96},{96,112},{1,17},{17... | collective-permute-start | bytes 1572872 | tf_op jit(solution)/shard_map/ppermute | solution.py:19
  229.0 15.3 %collective-permute-start.5 = (f32[2,128,512]{2,1,0:T(8,128)S(1)}, f32[2,128,512]{2,1,0:T(8,128)S(1)}, u32[]{:S(2)}, u32[]{:S(2)}) collective-permute-start(f32[2,128,512]{2,1,0:T(8,128)S(1)} %get-tuple-element.456), channel_id=1, source_target_pairs={{16,0},{32,16},{48,32},{64,48},{80,64},{96,80},{112,96},{17,1},{33... | collective-permute-start | bytes 1572872 | tf_op jit(solution)/shard_map/ppermute | solution.py:21
  240.2 0.8 copy-start.29
  241.2 13.8 %copy-start.10 = (f32[2,256,256]{2,1,0:T(8,128)S(1)}, f32[2,256,256]{2,1,0:T(8,128)}, u32[]{:S(2)}) copy-start(f32[2,256,256]{2,1,0:T(8,128)} %param.41) | copy-start | bytes 1572868
  244.3 1.3 copy-start.30
  244.3 13.3 %copy-start.34 = (f32[256,256]{0,1:T(8,128)S(1)}, f32[256,256]{0,1:T(8,128)}, u32[]{:S(2)}) copy-start(f32[256,256]{0,1:T(8,128)} %get-tuple-element.390) | copy-start | bytes 786436
  244.4 13.3 %copy-start.35 = (f32[256,256]{0,1:T(8,128)S(1)}, f32[256,256]{0,1:T(8,128)}, u32[]{:S(2)}) copy-start(f32[256,256]{0,1:T(8,128)} %get-tuple-element.391) | copy-start | bytes 786436
  245.6 26.5 %collective-permute-start.6 = (f32[2,768,128]{2,1,0:T(8,128)}, f32[2,768,128]{2,1,0:T(8,128)}, u32[]{:S(2)}, u32[]{:S(2)}) collective-permute-start(f32[2,768,128]{2,1,0:T(8,128)} %get-tuple-element.453), channel_id=1, source_target_pairs={{0,1},{1,2},{2,3},{3,4},{4,5},{5,6},{6,7},{7,8},{8,9},{9,10},{10,1... | collective-permute-start | bytes 2359304 | tf_op jit(solution)/shard_map/ppermute | solution.py:19
  255.7 17.4 %collective-permute-start.7 = (f32[2,768,128]{2,1,0:T(8,128)}, f32[2,768,128]{2,1,0:T(8,128)}, u32[]{:S(2)}, u32[]{:S(2)}) collective-permute-start(f32[2,768,128]{2,1,0:T(8,128)} %get-tuple-element.452), channel_id=1, source_target_pairs={{1,0},{2,1},{3,2},{4,3},{5,4},{6,5},{7,6},{8,7},{9,8},{10,9},{11,1... | collective-permute-start | bytes 2359304 | tf_op jit(solution)/shard_map/ppermute | solution.py:21
  258.5 516.3 %all-reduce.5.cloned.1.call-start = ((), (), s32[]{:S(2)}) async-start(), calls=%async_computation | async-start | bytes 1572864 | tf_op jit(solution)/shard_map/psum | solution.py:107
  259.5 22.6 %copy-start.9 = (f32[2,256,256]{2,1,0:T(8,128)S(1)}, f32[2,256,256]{2,1,0:T(8,128)}, u32[]{:S(2)}) copy-start(f32[2,256,256]{2,1,0:T(8,128)} %param.40) | copy-start | bytes 1572868
  282.7 149.8 %copy-start.2 = (f32[2,256,256]{2,1,0:T(8,128)}, f32[2,256,256]{2,1,0:T(8,128)S(1)}, u32[]{:S(2)}) copy-start(f32[2,256,256]{2,1,0:T(8,128)S(1)} %divide_add_fusion.3) | copy-start | bytes 1572868
  282.8 133.9 %collective-permute-start.8 = (f32[2,128,256]{2,1,0:T(8,128)S(1)}, f32[2,128,256]{2,1,0:T(8,128)S(1)}, u32[]{:S(2)}, u32[]{:S(2)}) collective-permute-start(f32[2,128,256]{2,1,0:T(8,128)S(1)} %get-tuple-element.464), channel_id=1, source_target_pairs={{0,16},{16,32},{32,48},{48,64},{64,80},{80,96},{96,112},{1,17},{17... | collective-permute-start | bytes 786440 | tf_op jit(solution)/shard_map/ppermute | solution.py:19
  289.2 127.4 %collective-permute-start.9 = (f32[2,128,256]{2,1,0:T(8,128)S(1)}, f32[2,128,256]{2,1,0:T(8,128)S(1)}, u32[]{:S(2)}, u32[]{:S(2)}) collective-permute-start(f32[2,128,256]{2,1,0:T(8,128)S(1)} %get-tuple-element.465), channel_id=1, source_target_pairs={{16,0},{32,16},{48,32},{64,48},{80,64},{96,80},{112,96},{17,1},{33... | collective-permute-start | bytes 786440 | tf_op jit(solution)/shard_map/ppermute | solution.py:21
  416.6 6.1 copy-start.31
  416.6 6.2 copy-start.42
  416.6 0.7 copy-start.38
  416.7 0.8 copy-start.40
  417.4 15.1 %copy-start.39 = (f32[2,128,256]{2,1,0:T(8,128)S(1)}, f32[2,128,256]{2,1,0:T(8,128)}, u32[]{:S(2)}) copy-start(f32[2,128,256]{2,1,0:T(8,128)} %copy-done.38) | copy-start | bytes 786436
  417.4 15.1 %copy-start.41 = (f32[2,128,256]{2,1,0:T(8,128)S(1)}, f32[2,128,256]{2,1,0:T(8,128)}, u32[]{:S(2)}) copy-start(f32[2,128,256]{2,1,0:T(8,128)} %copy-done.40) | copy-start | bytes 786436
  417.4 15.1 %collective-permute-start.10 = (f32[2,512,128]{2,1,0:T(8,128)S(1)}, f32[2,512,128]{2,1,0:T(8,128)S(1)}, u32[]{:S(2)}, u32[]{:S(2)}) collective-permute-start(f32[2,512,128]{2,1,0:T(8,128)S(1)} %get-tuple-element.458), channel_id=1, source_target_pairs={{0,1},{1,2},{2,3},{3,4},{4,5},{5,6},{6,7},{7,8},{8,9},{9,10},{10,1... | collective-permute-start | bytes 1572872 | tf_op jit(solution)/shard_map/ppermute | solution.py:19
  420.8 11.7 %collective-permute-start.11 = (f32[2,512,128]{2,1,0:T(8,128)S(1)}, f32[2,512,128]{2,1,0:T(8,128)S(1)}, u32[]{:S(2)}, u32[]{:S(2)}) collective-permute-start(f32[2,512,128]{2,1,0:T(8,128)S(1)} %get-tuple-element.459), channel_id=1, source_target_pairs={{1,0},{2,1},{3,2},{4,3},{5,4},{6,5},{7,6},{8,7},{9,8},{10,9},{11,1... | collective-permute-start | bytes 1572872 | tf_op jit(solution)/shard_map/ppermute | solution.py:21
  422.9 9.6 %copy-start.6 = (f32[2,256,256]{1,2,0:T(8,128)}, f32[2,256,256]{1,2,0:T(8,128)S(1)}, u32[]{:S(2)}) copy-start(f32[2,256,256]{1,2,0:T(8,128)S(1)} %divide_add_fusion.2) | copy-start | bytes 1572868
  460.2 2.9 copy-start.24
  460.2 2.9 copy-start.26
  463.1 7.6 copy-start.20
  463.2 7.6 copy-start.22
  470.7 7.4 copy-start.5
  478.1 1.1 copy-start.16
  478.1 1.2 copy-start.18
  479.3 7.6 copy-start.12
  479.3 7.6 copy-start.14
  487.0 7.4 copy-start.1
  487.0 7.4 copy-start.28
  617.8 3.1 copy-start.36
  617.9 3.1 copy-start.37
  617.9 5.3 copy-start.7
  618.9 158.0 %collective-permute-start.12 = (f32[2,128,512]{2,1,0:T(8,128)}, f32[2,128,512]{2,1,0:T(8,128)}, u32[]{:S(2)}, u32[]{:S(2)}) collective-permute-start(f32[2,128,512]{2,1,0:T(8,128)} %get-tuple-element.455), channel_id=1, source_target_pairs={{0,16},{16,32},{32,48},{48,64},{64,80},{80,96},{96,112},{1,17},{17... | collective-permute-start | bytes 1572872 | tf_op jit(solution)/shard_map/ppermute | solution.py:19
  621.9 156.4 %collective-permute-start.13 = (f32[2,128,512]{2,1,0:T(8,128)}, f32[2,128,512]{2,1,0:T(8,128)}, u32[]{:S(2)}, u32[]{:S(2)}) collective-permute-start(f32[2,128,512]{2,1,0:T(8,128)} %get-tuple-element.454), channel_id=1, source_target_pairs={{16,0},{32,16},{48,32},{64,48},{80,64},{96,80},{112,96},{17,1},{33... | collective-permute-start | bytes 1572872 | tf_op jit(solution)/shard_map/ppermute | solution.py:21
  778.2 5.6 copy-start.32
  779.4 6.5 copy-start.43
  780.6 20.9 %collective-permute-start.14 = (f32[2,768,128]{2,1,0:T(8,128)}, f32[2,768,128]{2,1,0:T(8,128)}, u32[]{:S(2)}, u32[]{:S(2)}) collective-permute-start(f32[2,768,128]{2,1,0:T(8,128)} %get-tuple-element.451), channel_id=1, source_target_pairs={{0,1},{1,2},{2,3},{3,4},{4,5},{5,6},{6,7},{7,8},{8,9},{9,10},{10,1... | collective-permute-start | bytes 2359304 | tf_op jit(solution)/shard_map/ppermute | solution.py:19
  783.9 18.6 %collective-permute-start.15 = (f32[2,768,128]{2,1,0:T(8,128)}, f32[2,768,128]{2,1,0:T(8,128)}, u32[]{:S(2)}, u32[]{:S(2)}) collective-permute-start(f32[2,768,128]{2,1,0:T(8,128)} %get-tuple-element.450), channel_id=1, source_target_pairs={{1,0},{2,1},{3,2},{4,3},{5,4},{6,5},{7,6},{8,7},{9,8},{10,9},{11,1... | collective-permute-start | bytes 2359304 | tf_op jit(solution)/shard_map/ppermute | solution.py:21
  789.8 21.7 %copy-start.3 = (f32[2,256,256]{2,1,0:T(8,128)S(1)}, f32[2,256,256]{2,1,0:T(8,128)}, u32[]{:S(2)}) copy-start(f32[2,256,256]{2,1,0:T(8,128)} %copy-done.2) | copy-start | bytes 1572868
Sparse Core Ops, SparseCore 0:
  258.6 155.6 all-reduce.6
  622.0 152.7 all-reduce.4
where the time goes:
time: 828 us; the launch traced here: 820 us
  waiting for transfers between devices  326 us (39%)
  local copies, waits for them, and re-layouts  250 us (30%)
  loops' own time  62.8 us (8%)
  matrix products  60 us (7%)
  other arithmetic  56.8 us (7%)
  starting transfers between devices  47.9 us (6%)
  between operations  16.6 us (2%)
    psum x2, waiting for transfers between devices, shards(): total_grad, total_weight = lax.psum((grad_probe, weight), ('gy', 'gx'))  274 us
    dynamic_update_slice x16, local copies, waits for them, and re-layouts, deposit(): lax.dynamic_update_slice(total, current + grads[item], (0, corner[0], cor...  141 us
    another operation x2, loops' own time, shards(): lax.fori_loop(0, count, deposit, jnp.zeros((2, extent, extent), jnp.float...  62.1 us
    gather x80, local copies, waits for them, and re-layouts  50.6 us
    ppermute x8, waiting for transfers between devices, with_halo(): lax.ppermute(tail, axis, [(i, (i + 1) % count) for i in range(ends)])  45.1 us
    ppermute x8, starting transfers between devices, with_halo(): lax.ppermute(tail, axis, [(i, (i + 1) % count) for i in range(ends)])  34.9 us
    dot_general x4, matrix products, transform(): jnp.einsum('abjk,pbkl->pajl', left, field, precision=lax.Precision.HIGHEST)  30.3 us
    dot_general x4, matrix products, transform(): jnp.einsum('pbjk,bakl->pajl', middle, right, precision=lax.Precision.HIGH...  29.7 us
  transfers between devices with their start and end apart: 18, of which 10 were waited for; matrix products, arithmetic and copies ran while one was open for 5% of the time, Pallas kernels for 0%

commit v1 on v0

v1 whole, which is shorter than its diff:
```python
import functools

import jax
import jax.numpy as jnp
import ml_dtypes
import numpy as np
from jax import lax
from jax.experimental import pallas as pl
from jax.experimental.pallas import tpu as pltpu
from jax.sharding import PartitionSpec as P

MESH = pl.DeviceIdType.MESH
F32 = jnp.float32
BF16 = jnp.bfloat16
VMEM = pl.BlockSpec(memory_space=pltpu.VMEM)
SMEM = pl.BlockSpec(memory_space=pltpu.SMEM)
VMEM_LIMIT = 60 * 1024 * 1024

DIRS = [(-1, 0), (1, 0), (0, -1), (0, 1), (-1, -1), (-1, 1), (1, -1), (1, 1)]


def tables():
    n = np.arange(128)[:, None]
    out = []
    for parity in range(2):
        turns = (n * (2 * np.arange(128)[None, :] + parity)) % 256
        angle = -2.0 * np.pi * turns / 256.0
        re, im = np.cos(angle) / 16.0, np.sin(angle) / 16.0
        m = np.block([[re, im], [-im, re]]).astype(np.float32)
        hi = m.astype(ml_dtypes.bfloat16)
        lo = (m - hi.astype(np.float32)).astype(ml_dtypes.bfloat16)
        out.append(np.stack([hi, lo]))
    right = np.stack(out)
    return right, np.ascontiguousarray(np.swapaxes(right, 2, 3))


def sorting():
    m = np.zeros((256, 256), np.float32)
    m[np.arange(256), np.concatenate([np.arange(0, 256, 2), np.arange(1, 256, 2)])] = 1.0
    return np.stack([m, m.T]).astype(ml_dtypes.bfloat16)


def neighbor(dy, dx):
    y = lax.axis_index("gy") + dy
    x = lax.axis_index("gx") + dx
    ny, nx = lax.axis_size("gy"), lax.axis_size("gx")
    ok = (y >= 0) & (y < ny) & (x >= 0) & (x < nx)
    return ok, (jnp.clip(y, 0, ny - 1), jnp.clip(x, 0, nx - 1))


def halo_region(dy, dx):
    rows = {-1: slice(0, 128), 0: slice(128, 384), 1: slice(384, 512)}[dy]
    cols = {-1: slice(0, 1), 0: slice(1, 3), 1: slice(3, 4)}[dx]
    return cols, rows


def edge_region(dy, dx):
    rows = {-1: slice(128, 256), 0: slice(128, 384), 1: slice(256, 384)}[dy]
    cols = {-1: slice(1, 2), 0: slice(1, 3), 1: slice(2, 3)}[dx]
    return cols, rows


def greet_sides():
    barrier = pltpu.get_barrier_semaphore()
    count = jnp.int32(0)
    for d in DIRS:
        ok, device = neighbor(*d)

        @pl.when(ok)
        def _(device=device):
            pl.semaphore_signal(barrier, inc=1, device_id=device, device_id_type=MESH)

        count = count + ok.astype(jnp.int32)
    return barrier, count


def side_copies(source, target, outward, send, recv):
    out = []
    for i, (dy, dx) in enumerate(DIRS):
        ok, device = neighbor(dy, dx)
        cols, rows = edge_region(dy, dx) if outward else halo_region(dy, dx)
        tcols, trows = halo_region(-dy, -dx) if outward else (cols, rows)
        out.append(
            (
                ok,
                neighbor(-dy, -dx)[0],
                pltpu.make_async_remote_copy(
                    source.at[:, cols, rows, :],
                    target.at[:, tcols, trows, :],
                    send.at[i],
                    recv.at[i],
                    device_id=device,
                    device_id_type=MESH,
                ),
            )
        )
    return out


def start_sides(copies):
    for ok, _, copy in copies:
        pl.when(ok)(copy.start)


def wait_sides(copies):
    for ok, arrives, copy in copies:
        pl.when(ok)(copy.wait_send)
        pl.when(arrives)(copy.wait_recv)


def blank_outside(ext):
    for dy, dx in DIRS:
        cols, rows = halo_region(dy, dx)

        @pl.when(jnp.logical_not(neighbor(dy, dx)[0]))
        def _(cols=cols, rows=rows):
            ext[:, cols, rows, :] = jnp.zeros((2, cols.stop - cols.start, rows.stop - rows.start, 128), F32)


def halo_kernel(obj, amps, sort, ext, amps_out, send, recv):
    blank_outside(ext)
    barrier, count = greet_sides()
    for b in range(2):
        ext[:, 1 + b, 128:384, :] = obj[:, :, 128 * b : 128 * b + 128]
    pl.semaphore_wait(barrier, count)
    copies = side_copies(ext, ext, True, send, recv)
    start_sides(copies)

    def arrange(k, carry):
        half = jnp.dot(sort[0], amps[k], preferred_element_type=F32).astype(BF16)
        amps_out[k] = jnp.dot(half, sort[1], preferred_element_type=F32).astype(BF16)
        return carry

    lax.fori_loop(0, amps.shape[0], arrange, jnp.int32(0))
    wait_sides(copies)


def split(x):
    hi = x.astype(BF16)
    return hi, (x - hi.astype(F32)).astype(BF16)


def right_dot(hi, lo, m):
    return jnp.dot(
        jnp.concatenate([hi, lo, hi], axis=1),
        jnp.concatenate([m[0], m[0], m[1]], axis=0),
        preferred_element_type=F32,
    )


def left_dot(m, hi, lo):
    return jnp.dot(
        jnp.concatenate([m[0], m[0], m[1]], axis=1),
        jnp.concatenate([hi, lo, hi], axis=0),
        preferred_element_type=F32,
    )


def compute_kernel(local, ext, probe, amps, right, left, grad, total, cut, lhs_hi, lhs_lo):
    grad[...] = jnp.zeros_like(grad)
    total[...] = jnp.zeros_like(total)
    lane = lax.broadcasted_iota(jnp.int32, (1, 128), 1)

    def visit(k, carry):
        r = local[k, 0]
        c = local[k, 1]
        first = lax.div(c, 128)
        c = lax.rem(c, 128)
        back = lax.rem(128 - c, 128)
        keep = lane < 128 - c
        late = lane >= c
        for i in range(0, 256, 64):
            rows = slice(i, i + 64)
            part = []
            for p in range(2):
                t = [pltpu.roll(ext[p, first + b, pl.ds(r + i, 64), :], back, 1) for b in range(3)]
                h = [jnp.where(keep, t[0], t[1]), jnp.where(keep, t[1], t[2])]
                for b in range(2):
                    cut[p, b, rows, :] = h[b]
                part.append(h)
            wave = []
            for b in range(2):
                ore, oim = part[0][b], part[1][b]
                pre, pim = probe[0, b, rows, :], probe[1, b, rows, :]
                total[2, b, rows, :] += ore * ore + oim * oim
                wave.append((pre * ore - pim * oim, pre * oim + pim * ore))
            for q in range(2):
                for p in range(2):
                    x = wave[0][p] + wave[1][p] if q == 0 else wave[0][p] - wave[1][p]
                    hi, lo = split(x)
                    lhs_hi[q, rows, 128 * p : 128 * p + 128] = hi
                    lhs_lo[q, rows, 128 * p : 128 * p + 128] = lo
        y = [right_dot(lhs_hi[q], lhs_lo[q], right[q]) for q in range(2)]
        half = []
        for s in range(2):
            pieces = []
            for p in range(2):
                lanes = slice(128 * p, 128 * p + 128)
                top = jnp.concatenate([y[0][:128, lanes], y[1][:128, lanes]], axis=1)
                low = jnp.concatenate([y[0][128:, lanes], y[1][128:, lanes]], axis=1)
                pieces.append(top + low if s == 0 else top - low)
            hi, lo = split(jnp.concatenate(pieces, axis=0))
            far = left_dot(left[s], hi, lo)
            re, im = far[:128], far[128:]
            factor = amps[k, 128 * s : 128 * s + 128, :].astype(F32) * lax.rsqrt(jnp.maximum(re * re + im * im, 0.25)) - 1.0
            hi, lo = split(jnp.concatenate([re * factor, im * factor], axis=0))
            half.append(left_dot(right[s], hi, lo))
        top, low = half[0] + half[1], half[0] - half[1]
        chi = []
        for q in range(2):
            lanes = slice(128 * q, 128 * q + 128)
            x = jnp.concatenate(
                [
                    jnp.concatenate([top[:128, lanes], top[128:, lanes]], axis=1),
                    jnp.concatenate([low[:128, lanes], low[128:, lanes]], axis=1),
                ],
                axis=0,
            )
            hi, lo = split(x)
            chi.append(right_dot(hi, lo, left[q]))
        for i in range(0, 256, 64):
            rows = slice(i, i + 64)
            g = [[], []]
            for b in range(2):
                x = chi[0][rows] + chi[1][rows] if b == 0 else chi[0][rows] - chi[1][rows]
                cre, cim = x[:, :128], x[:, 128:]
                pre, pim = probe[0, b, rows, :], probe[1, b, rows, :]
                ore, oim = cut[0, b, rows, :], cut[1, b, rows, :]
                total[0, b, rows, :] += ore * cre + oim * cim
                total[1, b, rows, :] += ore * cim - oim * cre
                g[0].append(pltpu.roll(pre * cre + pim * cim, c, 1))
                g[1].append(pltpu.roll(pre * cim - pim * cre, c, 1))
            for p in range(2):
                grad[p, first, pl.ds(r + i, 64), :] += jnp.where(late, g[p][0], 0.0)
                grad[p, first + 1, pl.ds(r + i, 64), :] += jnp.where(late, g[p][1], g[p][0])
                grad[p, first + 2, pl.ds(r + i, 64), :] += jnp.where(late, 0.0, g[p][1])
        return carry

    lax.fori_loop(0, amps.shape[0], visit, jnp.int32(0))


def group_ids():
    gy, gx = lax.axis_index("gy"), lax.axis_index("gx")
    return lax.rem(gx, 2), lax.rem(gy, 4), lax.div(gy, 4) * 8 + lax.div(gx, 2)


def sibling():
    gy, gx = lax.axis_index("gy"), lax.axis_index("gx")
    return gy, gx + 1 - 2 * lax.rem(gx, 2)


def along_y(d):
    gy, gx = lax.axis_index("gy"), lax.axis_index("gx")
    y = lax.rem(gy, 4)
    return gy - y + lax.rem(y + d, 4), gx


def member(j):
    gy, gx = lax.axis_index("gy"), lax.axis_index("gx")
    return lax.div(j, 8) * 4 + lax.rem(gy, 4), lax.rem(j, 8) * 2 + lax.rem(gx, 2)


class Sum:
    def __init__(self, total, full, acc0, acc1, acc2, rb0, rb1, rb2, sems):
        self.total, self.full, self.acc0, self.acc1, self.acc2 = total, full, acc0, acc1, acc2
        self.rb0, self.rb1, self.rb2 = rb0, rb1, rb2
        self.sems = sems
        self.core, self.y, self.me = group_ids()
        self.mine = lax.rem(self.me, 8)

    def greet(self, barrier):
        devices = [sibling()] + [along_y(d) for d in (1, 2, 3)] + [member(lax.rem(self.me + d, 16)) for d in range(1, 16)]
        for device in devices:
            pl.semaphore_signal(barrier, inc=1, device_id=device, device_id_type=MESH)
        return len(devices)

    def copy(self, source, target, i, j, device):
        send, recv = self.sems
        return pltpu.make_async_remote_copy(
            source, target, send.at[i], recv.at[j], device_id=device, device_id_type=MESH
        )

    def step0(self):
        theirs = pl.ds(pl.multiple_of((1 - self.core) * 128, 128), 128)
        self.c0 = self.copy(self.total.at[:, theirs, :], self.rb0, 0, 0, sibling())
        self.c0.start()

    def step1(self):
        self.c0.wait_recv()
        own = pl.ds(pl.multiple_of(self.core * 128, 128), 128)
        self.acc0[...] = self.total[:, own, :] + self.rb0[...]
        self.c1 = []
        for d in (1, 2, 3):
            part = pl.ds(pl.multiple_of(lax.rem(self.y + d, 4) * 32, 32), 32)
            c = self.copy(self.acc0.at[:, part, :], self.rb1.at[d - 1], d, d, along_y(d))
            c.start()
            self.c1.append(c)

    def step2(self):
        for c in self.c1:
            c.wait_recv()
        own = pl.ds(pl.multiple_of(self.y * 32, 32), 32)
        x = self.acc0[:, own, :] + self.rb1[0] + self.rb1[1] + self.rb1[2]
        self.acc1[...] = x.reshape(24, 8, 128)
        self.rb2[pl.ds(self.me, 1)] = self.acc1[pl.ds(self.mine * 3, 3)][None]
        self.c2 = []
        for d in range(1, 16):
            to = lax.rem(self.me + d, 16)
            c = self.copy(
                self.acc1.at[pl.ds(lax.rem(to, 8) * 3, 3)], self.rb2.at[self.me], 3 + d, 3 + d, member(to)
            )
            c.start()
            self.c2.append(c)

    def step3(self):
        for c in self.c2:
            c.wait_recv()
        x = self.rb2[0]
        for j in range(1, 16):
            x = x + self.rb2[j]
        self.acc2[...] = x
        place = self.full.at[self.core, self.y, pl.ds(self.mine * 3, 3)]
        self.full[pl.ds(self.core, 1), pl.ds(self.y, 1), pl.ds(self.mine * 3, 3)] = x[None, None]
        self.c3 = []
        for d in range(1, 8):
            to = lax.rem(self.mine + d, 8) + lax.div(self.me, 8) * 8
            c = self.copy(self.acc2, place, 18 + d, 18 + d, member(to))
            c.start()
            self.c3.append(c)

    def step4(self):
        for c in self.c3:
            c.wait_recv()
        self.c4 = []
        for d in (1, 2, 3):
            place = self.full.at[self.core, self.y]
            c = self.copy(place, place, 25 + d, 25 + d, along_y(d))
            c.start()
            self.c4.append(c)

    def step5(self):
        for c in self.c4:
            c.wait_recv()
        place = self.full.at[self.core]
        self.c5 = self.copy(place, place, 29, 29, sibling())
        self.c5.start()

    def finish(self):
        self.c5.wait_recv()
        for c in [self.c0, *self.c1, *self.c2, *self.c3, *self.c4, self.c5]:
            c.wait_send()


SUM_SCRATCH = [
    pltpu.VMEM((2, 4, 24, 8, 128), F32),
    pltpu.VMEM((6, 128, 128), F32),
    pltpu.VMEM((24, 8, 128), F32),
    pltpu.VMEM((3, 8, 128), F32),
    pltpu.VMEM((6, 128, 128), F32),
    pltpu.VMEM((3, 6, 32, 128), F32),
    pltpu.VMEM((16, 3, 8, 128), F32),
    pltpu.SemaphoreType.DMA((30,)),
    pltpu.SemaphoreType.DMA((30,)),
]


def new_probe(probe, full, write):
    weights = [full[h, y, 16:24] for h in range(2) for y in range(4)]
    top = weights[0]
    for w in weights[1:]:
        top = jnp.maximum(top, w)
    floor = 0.1 * jnp.max(top)
    for h in range(2):
        for y in range(4):
            rows = slice(128 * h + 32 * y, 128 * h + 32 * y + 32)
            for b in range(2):
                w = 0.9 * full[h, y, 16 + 4 * b : 20 + 4 * b].reshape(32, 128) + floor
                for p in range(2):
                    g = full[h, y, 8 * p + 4 * b : 8 * p + 4 * b + 4].reshape(32, 128)
                    write(p, b, rows, probe[p, b, rows, :] + g / w)


def step_kernel(last, ext, grad, total, probe, *refs):
    if last:
        obj_out, probe_out, inbox, acc, send, recv, *rest = refs
    else:
        ext_out, probe_out, inbox, acc, send, recv, send2, recv2, *rest = refs
    full, acc0, acc1, acc2, rb0, rb1, rb2, ssem, rsem = rest
    adder = Sum(total, full, acc0, acc1, acc2, rb0, rb1, rb2, (ssem, rsem))
    if not last:
        blank_outside(ext_out)
    barrier, count = greet_sides()
    count = count + adder.greet(barrier)
    pl.semaphore_wait(barrier, count)
    adder.step0()
    copies = side_copies(grad, inbox, False, send, recv)
    start_sides(copies)
    peak = jnp.max(probe[0] * probe[0] + probe[1] * probe[1])
    adder.step1()
    acc[...] = grad[:, 1:3, 128:384, :]
    adder.step2()
    wait_sides(copies)
    for i, (dy, dx) in enumerate(DIRS):
        cols, rows = halo_region(dy, dx)
        tcols, trows = edge_region(-dy, -dx)

        @pl.when(neighbor(-dy, -dx)[0])
        def _(cols=cols, rows=rows, tcols=tcols, trows=trows):
            acc[:, tcols.start - 1 : tcols.stop - 1, trows.start - 128 : trows.stop - 128, :] += inbox[:, cols, rows, :]

    if last:
        for b in range(2):
            obj_out[:, :, 128 * b : 128 * b + 128] = ext[:, 1 + b, 128:384, :] + acc[:, b] / peak
    else:
        ext_out[:, 1:3, 128:384, :] = ext[:, 1:3, 128:384, :] + acc[...] / peak
        copies = side_copies(ext_out, ext_out, True, send2, recv2)
        start_sides(copies)
    adder.step3()
    adder.step4()
    adder.step5()
    adder.finish()

    def write(p, b, rows, x):
        if last:
            probe_out[p, rows, 128 * b : 128 * b + 128] = x
        else:
            probe_out[p, b, rows, :] = x

    new_probe(probe, full, write)
    if not last:
        wait_sides(copies)


EXT = jax.ShapeDtypeStruct((2, 4, 512, 128), F32)
BLOCKS = jax.ShapeDtypeStruct((2, 2, 256, 128), F32)
TILE = jax.ShapeDtypeStruct((2, 256, 256), F32)


def params(collective=None):
    if collective is None:
        return pltpu.CompilerParams(vmem_limit_bytes=VMEM_LIMIT)
    return pltpu.CompilerParams(collective_id=collective, has_side_effects=True, vmem_limit_bytes=VMEM_LIMIT)


def shards(obj, probe, positions, amps):
    count = positions.shape[2]
    anchor = jnp.stack([lax.axis_index("gy") * 256, lax.axis_index("gx") * 256])
    local = positions.reshape(count, 2) - anchor[None, :] + 128
    right, left = (jnp.asarray(t) for t in tables())
    probe = jnp.transpose(probe.reshape(2, 256, 2, 128), (0, 2, 1, 3))
    sides = pltpu.SemaphoreType.DMA((8,))
    ext, arranged = pl.pallas_call(
        halo_kernel,
        out_shape=(EXT, jax.ShapeDtypeStruct((count, 256, 256), BF16)),
        in_specs=[VMEM] * 3,
        out_specs=(VMEM, VMEM),
        scratch_shapes=[sides, sides],
        compiler_params=params(0),
        name="halo",
    )(obj, amps.reshape(count, 256, 256), jnp.asarray(sorting()))
    for step in range(2):
        last = step == 1
        grad, total = pl.pallas_call(
            compute_kernel,
            out_shape=(EXT, jax.ShapeDtypeStruct((3, 2, 256, 128), F32)),
            in_specs=[SMEM] + [VMEM] * 5,
            out_specs=(VMEM, VMEM),
            scratch_shapes=[
                pltpu.VMEM((2, 2, 256, 128), F32),
                pltpu.VMEM((2, 256, 256), BF16),
                pltpu.VMEM((2, 256, 256), BF16),
            ],
            compiler_params=params(),
            name="gradient",
        )(local, ext, probe, arranged, right, left)
        outs = pl.pallas_call(
            functools.partial(step_kernel, last),
            out_shape=(TILE, TILE) if last else (EXT, BLOCKS),
            in_specs=[VMEM] * 4,
            out_specs=(VMEM, VMEM),
            scratch_shapes=[
                pltpu.VMEM(EXT.shape, F32),
                pltpu.VMEM(BLOCKS.shape, F32),
                *[sides] * (2 if last else 4),
                *SUM_SCRATCH,
            ],
            compiler_params=params(1 + step),
            name="update",
        )(ext, grad, total.reshape(6, 256, 128), probe)
        ext, probe = outs
    return (ext, probe)


def solution(mesh):
    in_specs = (
        P(None, "gy", "gx"),
        P(),
        P("gy", "gx", None, None),
        P("gy", "gx", None, None, None),
    )
    out_specs = (P(None, "gy", "gx"), P())
    return jax.shard_map(shards, mesh=mesh, in_specs=in_specs, out_specs=out_specs, check_vma=False)
```

time: 828 us -> 178 us (0.21)
  waiting for transfers between devices: 326 us -> 0 us
  local copies, waits for them, and re-layouts: 250 us -> 6.72 us
  Pallas kernels: 0 us -> 169 us
  loops' own time: 62.8 us -> 0 us
  matrix products: 60 us -> 0 us
  other arithmetic: 56.8 us -> 0.67 us
  starting transfers between devices: 47.9 us -> 0 us
  between operations: 16.6 us -> 0.67 us
    psum x2 -> x0, waiting for transfers between devices: 274 us -> none  [shards(): total_grad, total_weight = lax.psum((grad_probe, weight), ('gy', 'gx'))]
    pallas_call x0 -> x5, Pallas kernels: none -> 169 us  [the longest x2 104 us: shards(): pl.pallas_call(functools.partial(step_kernel, last), out_shape=(TILE, TIL...]
    dynamic_update_slice x16 -> x0, local copies, waits for them, and re-layouts: 141 us -> none  [deposit(): lax.dynamic_update_slice(total, current + grads[item], (0, corner[0], cor...]
    another operation x4 -> x0, loops' own time: 62.8 us -> none  [the longest x2 62.1 us: shards(): lax.fori_loop(0, count, deposit, jnp.zeros((2, extent, extent), jnp.float...]
    dot_general x8 -> x0, matrix products: 60 us -> none  [the longest x4 30.3 us: transform(): jnp.einsum('abjk,pbkl->pajl', left, field, precision=lax.Precision.HIGHEST)]
    ppermute x16 -> x0, waiting for transfers between devices: 51.9 us -> none  [the longest x8 45.1 us: with_halo(): lax.ppermute(tail, axis, [(i, (i + 1) % count) for i in range(ends)])]
    gather x80 -> x0, local copies, waits for them, and re-layouts: 50.6 us -> none
    ppermute x16 -> x0, starting transfers between devices: 47.8 us -> none  [the longest x8 34.9 us: with_halo(): lax.ppermute(tail, axis, [(i, (i + 1) % count) for i in range(ends)])]
  transfers between devices with their start and end apart: 18 -> 0, of which waited for: 10 -> 0; matrix products, arithmetic and copies ran while one was open for 5% -> 0% of each run, Pallas kernels for 0% -> 0%
where the time goes in v1:
time: 178 us; the launch traced here: 177 us
  Pallas kernels  169 us (95%)
  local copies, waits for them, and re-layouts  6.72 us (4%)
    pallas_call x2, Pallas kernels, shards(): pl.pallas_call(functools.partial(step_kernel, last), out_shape=(TILE, TIL...  104 us
    pallas_call x2, Pallas kernels, shards(): pl.pallas_call(compute_kernel, out_shape=(EXT, jax.ShapeDtypeStruct((3, 2...  40.8 us
    pallas_call x1, Pallas kernels, shards(): pl.pallas_call(halo_kernel, out_shape=(EXT, jax.ShapeDtypeStruct((count,...  24.7 us
    unnamed x3, local copies, waits for them, and re-layouts  4.97 us

profile of v1, /device:TPU:1, one launch (start us, length us, event | category | flops | bytes accessed | tf_op | source)
XLA Modules:
  0.0 177.3 jit_solution(1767272808508982456)
XLA Ops:
  0.6 0.1 pad_add_fusion
  0.7 0.8 copy.10
  1.5 0.6 subtract_add_fusion.local
  2.1 1.2 copy.11
  3.3 1.0 copy.12
  4.3 24.7 %halo.1 = (f32[2,4,512,128]{3,2,1,0:T(8,128)}, bf16[8,256,256]{2,1,0:T(8,128)(2,1)}) custom-call(f32[2,256,256]{2,1,0:T(8,128)} %obj.1, bf16[8,256,256]{2,1,0:T(8,128)(2,1)} %bitcast.11, bf16[2,256,256]{2,1,0:T(8,128)(2,1)} %constant.21.clone.sort), custom_call_target="tpu_custom_call" | custom-call | tf_op jit(solution)/shard_map/halo/pallas_call | solution.py:452
  29.0 20.4 %gradient.2 = (f32[2,4,512,128]{3,2,1,0:T(8,128)}, f32[3,2,256,128]{3,2,1,0:T(8,128)}) custom-call(s32[8,2]{1,0:T(8,128)} %subtract_add_fusion.local, f32[2,4,512,128]{3,2,1,0:T(8,128)} %get-tuple-element.10.ext, f32[2,2,256,128]{3,2,1,0:T(8,128)} %bitcast.8, bf16[8,256,256]{2,1,0:T(8,128)(2,1)} %get-tuple-element.11.amps, ...), custom_call_target="tpu_custom_call" | custom-call | tf_op jit(solution)/shard_map/gradient/pallas_call | solution.py:463
  49.4 60.0 %update.2 = (f32[2,4,512,128]{3,2,1,0:T(8,128)}, f32[2,2,256,128]{3,2,1,0:T(8,128)}) custom-call(f32[2,4,512,128]{3,2,1,0:T(8,128)} %get-tuple-element.10.ext, f32[2,4,512,128]{3,2,1,0:T(8,128)} %get-tuple-element.12.grad, f32[6,256,128]{2,1,0:T(8,128)} %bitcast.13, f32[2,2,256,128]{3,2,1,0:T(8,128)} %bitcast.9), custom_call_target="tpu_custom_call" | custom-call | tf_op jit(solution)/shard_map/update/pallas_call | solution.py:476
  109.4 20.4 %gradient.3 = (f32[2,4,512,128]{3,2,1,0:T(8,128)}, f32[3,2,256,128]{3,2,1,0:T(8,128)}) custom-call(s32[8,2]{1,0:T(8,128)} %subtract_add_fusion.local, f32[2,4,512,128]{3,2,1,0:T(8,128)} %get-tuple-element.14.ext, f32[2,2,256,128]{3,2,1,0:T(8,128)} %get-tuple-element.15.probe, bf16[8,256,256]{2,1,0:T(8,128)(2,1)} %get-tuple-element.11.amps, ...), custom_call_target="tpu_custom_call" | custom-call | tf_op jit(solution)/shard_map/gradient/pallas_call | solution.py:463
  129.8 43.8 %update.3 = (f32[2,256,256]{2,1,0:T(8,128)}, f32[2,256,256]{2,1,0:T(8,128)}) custom-call(f32[2,4,512,128]{3,2,1,0:T(8,128)} %get-tuple-element.14.ext, f32[2,4,512,128]{3,2,1,0:T(8,128)} %get-tuple-element.16.grad, f32[6,256,128]{2,1,0:T(8,128)} %bitcast.12, f32[2,2,256,128]{3,2,1,0:T(8,128)} %get-tuple-element.15.probe), custom_call_target="tpu_custom_call" | custom-call | tf_op jit(solution)/shard_map/update/pallas_call | solution.py:476
  173.6 1.9 %copy.15 = f32[2,256,256]{2,1,0:T(8,128)} copy(f32[2,256,256]{2,1,0:T(8,128)} %get-tuple-element.20) | data formatting | bytes 1048576
  175.5 1.9 %copy.16 = f32[2,256,256]{2,1,0:T(8,128)} copy(f32[2,256,256]{2,1,0:T(8,128)} %get-tuple-element.21) | data formatting | bytes 1048576

commit v2 on v1

--- a/solution.py
+++ b/solution.py
@@ -117,22 +117,13 @@
             ext[:, cols, rows, :] = jnp.zeros((2, cols.stop - cols.start, rows.stop - rows.start, 128), F32)
 
 
-def halo_kernel(obj, amps, sort, ext, amps_out, send, recv):
-    blank_outside(ext)
-    barrier, count = greet_sides()
-    for b in range(2):
-        ext[:, 1 + b, 128:384, :] = obj[:, :, 128 * b : 128 * b + 128]
-    pl.semaphore_wait(barrier, count)
-    copies = side_copies(ext, ext, True, send, recv)
-    start_sides(copies)
-
-    def arrange(k, carry):
-        half = jnp.dot(sort[0], amps[k], preferred_element_type=F32).astype(BF16)
-        amps_out[k] = jnp.dot(half, sort[1], preferred_element_type=F32).astype(BF16)
+def arrange(amps, sort, out):
+    def one(k, carry):
+        half = jnp.dot(sort[0], amps[0, 0, k], preferred_element_type=F32).astype(BF16)
+        out[k] = jnp.dot(half, sort[1], preferred_element_type=F32).astype(BF16)
         return carry
 
-    lax.fori_loop(0, amps.shape[0], arrange, jnp.int32(0))
-    wait_sides(copies)
+    lax.fori_loop(0, out.shape[0], one, jnp.int32(0))
 
 
 def split(x):
@@ -156,14 +147,18 @@
     )
 
 
-def compute_kernel(local, ext, probe, amps, right, left, grad, total, cut, lhs_hi, lhs_lo):
-    grad[...] = jnp.zeros_like(grad)
+def gradients(positions, ext, probe, amps, right, left, grad, total, cut, lhs_hi, lhs_lo, stage):
     total[...] = jnp.zeros_like(total)
+    row0 = lax.axis_index("gy") * 256 - 128
+    col0 = lax.axis_index("gx") * 256 - 128
+
+    def corner(k):
+        return jnp.clip(positions[0, 0, k, 0] - row0, 0, 255), jnp.clip(positions[0, 0, k, 1] - col0, 0, 255)
+
     lane = lax.broadcasted_iota(jnp.int32, (1, 128), 1)
 
     def visit(k, carry):
-        r = local[k, 0]
-        c = local[k, 1]
+        r, c = corner(k)
         first = lax.div(c, 128)
         c = lax.rem(c, 128)
         back = lax.rem(128 - c, 128)
@@ -182,7 +177,7 @@
             for b in range(2):
                 ore, oim = part[0][b], part[1][b]
                 pre, pim = probe[0, b, rows, :], probe[1, b, rows, :]
-                total[2, b, rows, :] += ore * ore + oim * oim
+                total[4 + b, rows, :] += ore * ore + oim * oim
                 wave.append((pre * ore - pim * oim, pre * oim + pim * ore))
             for q in range(2):
                 for p in range(2):
@@ -226,17 +221,32 @@
                 cre, cim = x[:, :128], x[:, 128:]
                 pre, pim = probe[0, b, rows, :], probe[1, b, rows, :]
                 ore, oim = cut[0, b, rows, :], cut[1, b, rows, :]
-                total[0, b, rows, :] += ore * cre + oim * cim
-                total[1, b, rows, :] += ore * cim - oim * cre
+                total[b, rows, :] += ore * cre + oim * cim
+                total[2 + b, rows, :] += ore * cim - oim * cre
                 g[0].append(pltpu.roll(pre * cre + pim * cim, c, 1))
                 g[1].append(pltpu.roll(pre * cim - pim * cre, c, 1))
             for p in range(2):
-                grad[p, first, pl.ds(r + i, 64), :] += jnp.where(late, g[p][0], 0.0)
-                grad[p, first + 1, pl.ds(r + i, 64), :] += jnp.where(late, g[p][1], g[p][0])
-                grad[p, first + 2, pl.ds(r + i, 64), :] += jnp.where(late, 0.0, g[p][1])
+                place = slice(256 + i, 320 + i)
+                stage[k, p, 1, place, :] = jnp.where(late, g[p][0], 0.0)
+                stage[k, p, 2, place, :] = jnp.where(late, g[p][1], g[p][0])
+                stage[k, p, 3, place, :] = jnp.where(late, 0.0, g[p][1])
         return carry
 
     lax.fori_loop(0, amps.shape[0], visit, jnp.int32(0))
+
+    def gather(i, carry):
+        start = pl.multiple_of(i * 64, 64)
+        for p in range(2):
+            for b in range(4):
+                x = jnp.zeros((64, 128), F32)
+                for k in range(amps.shape[0]):
+                    r, c = corner(k)
+                    first = lax.div(c, 128)
+                    x = x + stage[k, p, b + 1 - first, pl.ds(256 + start - r, 64), :]
+                grad[p, b, pl.ds(start, 64), :] = x
+        return carry
+
+    lax.fori_loop(0, 8, gather, jnp.int32(0))
 
 
 def group_ids():
@@ -380,115 +390,109 @@
                     write(p, b, rows, probe[p, b, rows, :] + g / w)
 
 
-def step_kernel(last, ext, grad, total, probe, *refs):
-    if last:
-        obj_out, probe_out, inbox, acc, send, recv, *rest = refs
-    else:
-        ext_out, probe_out, inbox, acc, send, recv, send2, recv2, *rest = refs
-    full, acc0, acc1, acc2, rb0, rb1, rb2, ssem, rsem = rest
-    adder = Sum(total, full, acc0, acc1, acc2, rb0, rb1, rb2, (ssem, rsem))
-    if not last:
-        blank_outside(ext_out)
+def kernel(positions, obj, probe, amps, right, left, sort, obj_out, probe_out, *refs):
+    ext, grad, total, acc, probes, arranged, cut, lhs_hi, lhs_lo, stage, inbox, send, recv, *rest = refs
+    sums = []
+    for step in range(2):
+        parts = rest[len(SUM_SCRATCH) * step : len(SUM_SCRATCH) * (step + 1)]
+        sums.append(Sum(total, *parts[:-2], parts[-2:]))
+    for step in range(2):
+        blank_outside(ext.at[step])
     barrier, count = greet_sides()
-    count = count + adder.greet(barrier)
+    count = count + sums[0].greet(barrier)
+    for b in range(2):
+        lanes = slice(128 * b, 128 * b + 128)
+        ext[0, :, 1 + b, 128:384, :] = obj[:, :, lanes]
+        probes[0, :, b] = probe[:, :, lanes]
     pl.semaphore_wait(barrier, count)
-    adder.step0()
-    copies = side_copies(grad, inbox, False, send, recv)
+    copies = side_copies(ext.at[0], ext.at[0], True, send.at[0], recv.at[0])
     start_sides(copies)
-    peak = jnp.max(probe[0] * probe[0] + probe[1] * probe[1])
-    adder.step1()
-    acc[...] = grad[:, 1:3, 128:384, :]
-    adder.step2()
+    arrange(amps, sort, arranged)
+
+    def clear(k, carry):
+        for p in range(2):
+            for b in range(5):
+                for rows in (slice(0, 256), slice(256, 512), slice(512, 768)):
+                    if b in (0, 4) or rows.start != 256:
+                        stage[k, p, b, rows, :] = jnp.zeros((256, 128), F32)
+        return carry
+
+    lax.fori_loop(0, stage.shape[0], clear, jnp.int32(0))
     wait_sides(copies)
-    for i, (dy, dx) in enumerate(DIRS):
-        cols, rows = halo_region(dy, dx)
-        tcols, trows = edge_region(-dy, -dx)
-
-        @pl.when(neighbor(-dy, -dx)[0])
-        def _(cols=cols, rows=rows, tcols=tcols, trows=trows):
-            acc[:, tcols.start - 1 : tcols.stop - 1, trows.start - 128 : trows.stop - 128, :] += inbox[:, cols, rows, :]
-
-    if last:
-        for b in range(2):
-            obj_out[:, :, 128 * b : 128 * b + 128] = ext[:, 1 + b, 128:384, :] + acc[:, b] / peak
-    else:
-        ext_out[:, 1:3, 128:384, :] = ext[:, 1:3, 128:384, :] + acc[...] / peak
-        copies = side_copies(ext_out, ext_out, True, send2, recv2)
+    for step in range(2):
+        adder = sums[step]
+        old, now = ext.at[step], probes.at[step]
+        gradients(positions, old, now, arranged, right, left, grad, total, cut, lhs_hi, lhs_lo, stage)
+        adder.step0()
+        copies = side_copies(grad, inbox.at[step], False, send.at[1 + 2 * step], recv.at[1 + 2 * step])
         start_sides(copies)
-    adder.step3()
-    adder.step4()
-    adder.step5()
-    adder.finish()
-
-    def write(p, b, rows, x):
-        if last:
-            probe_out[p, rows, 128 * b : 128 * b + 128] = x
+        peak = jnp.max(now[0] * now[0] + now[1] * now[1])
+        adder.step1()
+        acc[...] = grad[:, 1:3, 128:384, :]
+        adder.step2()
+        wait_sides(copies)
+        for dy, dx in DIRS:
+            cols, rows = halo_region(dy, dx)
+            tcols, trows = edge_region(-dy, -dx)
+
+            @pl.when(neighbor(-dy, -dx)[0])
+            def _(cols=cols, rows=rows, tcols=tcols, trows=trows):
+                place = (slice(None), slice(tcols.start - 1, tcols.stop - 1), slice(trows.start - 128, trows.stop - 128))
+                acc[place] += inbox[step, :, cols, rows, :]
+
+        if step == 1:
+            for b in range(2):
+                obj_out[:, :, 128 * b : 128 * b + 128] = old[:, 1 + b, 128:384, :] + acc[:, b] / peak
         else:
-            probe_out[p, b, rows, :] = x
-
-    new_probe(probe, full, write)
-    if not last:
-        wait_sides(copies)
-
-
-EXT = jax.ShapeDtypeStruct((2, 4, 512, 128), F32)
-BLOCKS = jax.ShapeDtypeStruct((2, 2, 256, 128), F32)
-TILE = jax.ShapeDtypeStruct((2, 256, 256), F32)
-
-
-def params(collective=None):
-    if collective is None:
-        return pltpu.CompilerParams(vmem_limit_bytes=VMEM_LIMIT)
-    return pltpu.CompilerParams(collective_id=collective, has_side_effects=True, vmem_limit_bytes=VMEM_LIMIT)
+            ext[1, :, 1:3, 128:384, :] = old[:, 1:3, 128:384, :] + acc[...] / peak
+            copies = side_copies(ext.at[1], ext.at[1], True, send.at[2], recv.at[2])
+            start_sides(copies)
+        adder.step3()
+        adder.step4()
+        adder.step5()
+        adder.finish()
+
+        def write(p, b, rows, x):
+            if step == 1:
+                probe_out[p, rows, 128 * b : 128 * b + 128] = x
+            else:
+                probes[1, p, b, rows, :] = x
+
+        new_probe(now, adder.full, write)
+        if step == 0:
+            wait_sides(copies)
 
 
 def shards(obj, probe, positions, amps):
     count = positions.shape[2]
-    anchor = jnp.stack([lax.axis_index("gy") * 256, lax.axis_index("gx") * 256])
-    local = positions.reshape(count, 2) - anchor[None, :] + 128
     right, left = (jnp.asarray(t) for t in tables())
-    probe = jnp.transpose(probe.reshape(2, 256, 2, 128), (0, 2, 1, 3))
-    sides = pltpu.SemaphoreType.DMA((8,))
-    ext, arranged = pl.pallas_call(
-        halo_kernel,
-        out_shape=(EXT, jax.ShapeDtypeStruct((count, 256, 256), BF16)),
-        in_specs=[VMEM] * 3,
+    tile = jax.ShapeDtypeStruct((2, 256, 256), F32)
+    ext = (2, 4, 512, 128)
+    return pl.pallas_call(
+        kernel,
+        out_shape=(tile, tile),
+        in_specs=[SMEM] + [VMEM] * 6,
         out_specs=(VMEM, VMEM),
-        scratch_shapes=[sides, sides],
-        compiler_params=params(0),
-        name="halo",
-    )(obj, amps.reshape(count, 256, 256), jnp.asarray(sorting()))
-    for step in range(2):
-        last = step == 1
-        grad, total = pl.pallas_call(
-            compute_kernel,
-            out_shape=(EXT, jax.ShapeDtypeStruct((3, 2, 256, 128), F32)),
-            in_specs=[SMEM] + [VMEM] * 5,
-            out_specs=(VMEM, VMEM),
-            scratch_shapes=[
-                pltpu.VMEM((2, 2, 256, 128), F32),
-                pltpu.VMEM((2, 256, 256), BF16),
-                pltpu.VMEM((2, 256, 256), BF16),
-            ],
-            compiler_params=params(),
-            name="gradient",
-        )(local, ext, probe, arranged, right, left)
-        outs = pl.pallas_call(
-            functools.partial(step_kernel, last),
-            out_shape=(TILE, TILE) if last else (EXT, BLOCKS),
-            in_specs=[VMEM] * 4,
-            out_specs=(VMEM, VMEM),
-            scratch_shapes=[
-                pltpu.VMEM(EXT.shape, F32),
-                pltpu.VMEM(BLOCKS.shape, F32),
-                *[sides] * (2 if last else 4),
-                *SUM_SCRATCH,
-            ],
-            compiler_params=params(1 + step),
-            name="update",
-        )(ext, grad, total.reshape(6, 256, 128), probe)
-        ext, probe = outs
-    return (ext, probe)
+        scratch_shapes=[
+            pltpu.VMEM((2, *ext), F32),
+            pltpu.VMEM(ext, F32),
+            pltpu.VMEM((6, 256, 128), F32),
+            pltpu.VMEM((2, 2, 256, 128), F32),
+            pltpu.VMEM((2, 2, 2, 256, 128), F32),
+            pltpu.VMEM((count, 256, 256), BF16),
+            pltpu.VMEM((2, 2, 256, 128), F32),
+            pltpu.VMEM((2, 256, 256), BF16),
+            pltpu.VMEM((2, 256, 256), BF16),
+            pltpu.VMEM((count, 2, 5, 768, 128), F32),
+            pltpu.VMEM((2, *ext), F32),
+            pltpu.SemaphoreType.DMA((4, 8)),
+            pltpu.SemaphoreType.DMA((4, 8)),
+            *SUM_SCRATCH,
+            *SUM_SCRATCH,
+        ],
+        compiler_params=pltpu.CompilerParams(collective_id=0, has_side_effects=True, vmem_limit_bytes=VMEM_LIMIT),
+        name="iterations",
+    )(positions, obj, probe, amps, right, left, jnp.asarray(sorting()))
 
 
 def solution(mesh):

time: 178 us -> 153 us (0.86)
  Pallas kernels: 169 us -> 148 us
  local copies, waits for them, and re-layouts: 6.72 us -> 4.07 us
    pallas_call x5 -> x1, Pallas kernels: 169 us -> 148 us  [shards(): pl.pallas_call(kernel, out_shape=(tile, tile), in_specs=[SMEM] + [VMEM] *...]
    unnamed x3 -> x5, local copies, waits for them, and re-layouts: 4.97 us -> 4.07 us
where the time goes in v2:
time: 153 us
  Pallas kernels  148 us (97%)
  local copies, waits for them, and re-layouts  4.07 us (3%)
    pallas_call x1, Pallas kernels, shards(): pl.pallas_call(kernel, out_shape=(tile, tile), in_specs=[SMEM] + [VMEM] *...  148 us
    unnamed x5, local copies, waits for them, and re-layouts  4.07 us

profile of v2, /device:TPU:1, one launch (start us, length us, event | category | flops | bytes accessed | tf_op | source)
XLA Modules:
  0.0 152.7 jit_solution(7207806261930836435)
XLA Ops:
  0.6 1.3 copy.9.positions
  2.0 147.9 %iterations.1 = (f32[2,256,256]{2,1,0:T(8,128)}, f32[2,256,256]{2,1,0:T(8,128)}) custom-call(s32[1,1,8,2]{3,2,1,0:T(8,128)} %copy.9.positions, f32[2,256,256]{2,1,0:T(8,128)} %obj.1, f32[2,256,256]{2,1,0:T(8,128)} %probe.1, bf16[1,1,8,256,256]{4,3,2,1,0:T(8,128)(2,1)} %amps.1, bf16[2,2,256,256]{3,2,1,0:T(8,128)(2,1)} %constant.6.clone.right, ...), custom_call_target="tpu_custom_call" | custom-call | tf_op jit(solution)/shard_map/iterations/pallas_call | solution.py:471
  149.9 0.0 copy-start
  149.9 1.9 %copy.12 = f32[2,256,256]{2,1,0:T(8,128)} copy(f32[2,256,256]{2,1,0:T(8,128)} %get-tuple-element.4) | data formatting | bytes 1048576
  151.9 0.0 copy-done
  151.9 0.8 copy.13
Async XLA Ops:
  149.9 1.9 %copy-start = (f32[2,256,256]{2,1,0:T(8,128)S(1)}, f32[2,256,256]{2,1,0:T(8,128)}, u32[]{:S(2)}) copy-start(f32[2,256,256]{2,1,0:T(8,128)} %get-tuple-element.5) | copy-start | bytes 1572868

commit v3 on v2

v3 whole, which is shorter than its diff:
```python
import functools

import jax
import jax.numpy as jnp
import ml_dtypes
import numpy as np
from jax import lax
from jax.experimental import pallas as pl
from jax.experimental.pallas import tpu as pltpu
from jax.sharding import PartitionSpec as P

MESH = pl.DeviceIdType.MESH
F32 = jnp.float32
BF16 = jnp.bfloat16
VMEM = pl.BlockSpec(memory_space=pltpu.VMEM)
SMEM = pl.BlockSpec(memory_space=pltpu.SMEM)
VMEM_LIMIT = 60 * 1024 * 1024

DIRS = [(-1, 0), (1, 0), (0, -1), (0, 1), (-1, -1), (-1, 1), (1, -1), (1, 1)]


def tables():
    n = np.arange(128)[:, None]
    out = []
    for parity in range(2):
        turns = (n * (2 * np.arange(128)[None, :] + parity)) % 256
        angle = -2.0 * np.pi * turns / 256.0
        re, im = np.cos(angle) / 16.0, np.sin(angle) / 16.0
        m = np.block([[re, im], [-im, re]]).astype(np.float32)
        hi = m.astype(ml_dtypes.bfloat16)
        lo = (m - hi.astype(np.float32)).astype(ml_dtypes.bfloat16)
        out.append(np.stack([hi, lo]))
    right = np.stack(out)
    return right, np.ascontiguousarray(np.swapaxes(right, 2, 3))


def sorting():
    m = np.zeros((256, 256), np.float32)
    m[np.arange(256), np.concatenate([np.arange(0, 256, 2), np.arange(1, 256, 2)])] = 1.0
    return np.stack([m, m.T]).astype(ml_dtypes.bfloat16)


def neighbor(dy, dx):
    y = lax.axis_index("gy") + dy
    x = lax.axis_index("gx") + dx
    ny, nx = lax.axis_size("gy"), lax.axis_size("gx")
    ok = (y >= 0) & (y < ny) & (x >= 0) & (x < nx)
    return ok, (jnp.clip(y, 0, ny - 1), jnp.clip(x, 0, nx - 1))


def halo_region(dy, dx):
    rows = {-1: slice(0, 128), 0: slice(128, 384), 1: slice(384, 512)}[dy]
    cols = {-1: slice(0, 1), 0: slice(1, 3), 1: slice(3, 4)}[dx]
    return cols, rows


def edge_region(dy, dx):
    rows = {-1: slice(128, 256), 0: slice(128, 384), 1: slice(256, 384)}[dy]
    cols = {-1: slice(1, 2), 0: slice(1, 3), 1: slice(2, 3)}[dx]
    return cols, rows


def greet_sides():
    barrier = pltpu.get_barrier_semaphore()
    count = jnp.int32(0)
    for d in DIRS:
        ok, device = neighbor(*d)

        @pl.when(ok)
        def _(device=device):
            pl.semaphore_signal(barrier, inc=1, device_id=device, device_id_type=MESH)

        count = count + ok.astype(jnp.int32)
    return barrier, count


def side_copies(source, target, outward, send, recv):
    out = []
    for i, (dy, dx) in enumerate(DIRS):
        ok, device = neighbor(dy, dx)
        cols, rows = edge_region(dy, dx) if outward else halo_region(dy, dx)
        tcols, trows = halo_region(-dy, -dx) if outward else (cols, rows)
        out.append(
            (
                ok,
                neighbor(-dy, -dx)[0],
                pltpu.make_async_remote_copy(
                    source.at[:, cols, rows, :],
                    target.at[:, tcols, trows, :],
                    send.at[i],
                    recv.at[i],
                    device_id=device,
                    device_id_type=MESH,
                ),
            )
        )
    return out


def start_sides(copies):
    for ok, _, copy in copies:
        pl.when(ok)(copy.start)


def wait_sides(copies):
    for ok, arrives, copy in copies:
        pl.when(ok)(copy.wait_send)
        pl.when(arrives)(copy.wait_recv)


def blank_outside(ext):
    for dy, dx in DIRS:
        cols, rows = halo_region(dy, dx)

        @pl.when(jnp.logical_not(neighbor(dy, dx)[0]))
        def _(cols=cols, rows=rows):
            ext[:, cols, rows, :] = jnp.zeros((2, cols.stop - cols.start, rows.stop - rows.start, 128), F32)


def arrange(amps, sort, out):
    def one(k, carry):
        half = jnp.dot(sort[0], amps[0, 0, k], preferred_element_type=F32).astype(BF16)
        out[k] = jnp.dot(half, sort[1], preferred_element_type=F32).astype(BF16)
        return carry

    lax.fori_loop(0, out.shape[0], one, jnp.int32(0))


def split(x):
    hi = x.astype(BF16)
    return hi, (x - hi.astype(F32)).astype(BF16)


def right_dot(hi, lo, m):
    return jnp.dot(
        jnp.concatenate([hi, lo, hi], axis=1),
        jnp.concatenate([m[0], m[0], m[1]], axis=0),
        preferred_element_type=F32,
    )


def left_dot(m, hi, lo):
    return jnp.dot(
        jnp.concatenate([m[0], m[0], m[1]], axis=1),
        jnp.concatenate([hi, lo, hi], axis=0),
        preferred_element_type=F32,
    )


def corner(positions, k):
    row = positions[0, 0, k, 0] - lax.axis_index("gy") * 256 + 128
    col = positions[0, 0, k, 1] - lax.axis_index("gx") * 256 + 128
    return jnp.clip(row, 0, 255), jnp.clip(col, 0, 255)


def cut_patches(positions, ext, cut, total):
    total[4:6] = jnp.zeros((2, 256, 128), F32)
    lane = lax.broadcasted_iota(jnp.int32, (1, 128), 1)

    def visit(k, carry):
        r, c = corner(positions, k)
        first = lax.div(c, 128)
        c = lax.rem(c, 128)
        back = lax.rem(128 - c, 128)
        keep = lane < 128 - c
        for i in range(0, 256, 64):
            rows = slice(i, i + 64)
            part = []
            for p in range(2):
                t = [pltpu.roll(ext[p, first + b, pl.ds(r + i, 64), :], back, 1) for b in range(3)]
                h = [jnp.where(keep, t[0], t[1]), jnp.where(keep, t[1], t[2])]
                for b in range(2):
                    cut[k, p, b, rows, :] = h[b]
                part.append(h)
            for b in range(2):
                total[4 + b, rows, :] += part[0][b] * part[0][b] + part[1][b] * part[1][b]
        return carry

    lax.fori_loop(0, cut.shape[0], visit, jnp.int32(0))


def gradients(positions, cut, probe, amps, right, left, total, lhs_hi, lhs_lo, chi, stage):
    total[0:4] = jnp.zeros((4, 256, 128), F32)
    chi[...] = jnp.zeros_like(chi)
    lane = lax.broadcasted_iota(jnp.int32, (1, 128), 1)
    pairs = cut.shape[0] // 2

    def waves(k, u):
        for i in range(0, 256, 64):
            rows = slice(i, i + 64)
            place = slice(256 * u + i, 256 * u + i + 64)
            wave = []
            for b in range(2):
                ore, oim = cut[k, 0, b, rows, :], cut[k, 1, b, rows, :]
                pre, pim = probe[0, b, rows, :], probe[1, b, rows, :]
                wave.append((pre * ore - pim * oim, pre * oim + pim * ore))
            for q in range(2):
                for p in range(2):
                    x = wave[0][p] + wave[1][p] if q == 0 else wave[0][p] - wave[1][p]
                    hi, lo = split(x)
                    lhs_hi[q, place, 128 * p : 128 * p + 128] = hi
                    lhs_lo[q, place, 128 * p : 128 * p + 128] = lo

    def correct(k, s, top, low):
        hi, lo = split(top + low if s == 0 else top - low)
        far = left_dot(left[s], hi, lo)
        re, im = far[:128], far[128:]
        factor = amps[k, 128 * s : 128 * s + 128, :].astype(F32) * lax.rsqrt(jnp.maximum(re * re + im * im, 0.25)) - 1.0
        hi, lo = split(jnp.concatenate([re * factor, im * factor], axis=0))
        return left_dot(right[s], hi, lo)

    def deposit(k, u):
        c = lax.rem(corner(positions, k)[1], 128)
        late = lane >= c
        for i in range(0, 256, 64):
            rows = slice(i, i + 64)
            place = slice(256 * u + i, 256 * u + i + 64)
            even, odd = chi[0, place, :], chi[1, place, :]
            g = [[], []]
            for b in range(2):
                x = even + odd if b == 0 else even - odd
                cre, cim = x[:, :128], x[:, 128:]
                pre, pim = probe[0, b, rows, :], probe[1, b, rows, :]
                ore, oim = cut[k, 0, b, rows, :], cut[k, 1, b, rows, :]
                total[b, rows, :] += ore * cre + oim * cim
                total[2 + b, rows, :] += ore * cim - oim * cre
                g[0].append(pltpu.roll(pre * cre + pim * cim, c, 1))
                g[1].append(pltpu.roll(pre * cim - pim * cre, c, 1))
            for p in range(2):
                to = pl.ds(pl.multiple_of(512 * k + 256 + i, 64), 64)
                stage[p, 1, to, :] = jnp.where(late, g[p][0], 0.0)
                stage[p, 2, to, :] = jnp.where(late, g[p][1], g[p][0])
                stage[p, 3, to, :] = jnp.where(late, 0.0, g[p][1])

    def stack(y, u):
        out = []
        for h in range(2):
            rows = slice(256 * u + 128 * h, 256 * u + 128 * h + 128)
            parts = [
                jnp.concatenate([y[0][rows, lanes], y[1][rows, lanes]], axis=1)
                for lanes in (slice(0, 128), slice(128, 256))
            ]
            out.append(jnp.concatenate(parts, axis=0))
        return out

    def visit(j, carry):
        y = [right_dot(lhs_hi[q], lhs_lo[q], right[q]) for q in range(2)]
        for u in range(2):
            deposit(2 * jnp.maximum(j - 1, 0) + u, u)
        half = [[], []]
        for s in range(2):
            for u in range(2):
                top, low = stack(y, u)
                half[u].append(correct(2 * j + u, s, top, low))
        for q in range(2):
            lanes = slice(128 * q, 128 * q + 128)
            parts = []
            for u in range(2):
                for x in (half[u][0] + half[u][1], half[u][0] - half[u][1]):
                    parts.append(jnp.concatenate([x[:128, lanes], x[128:, lanes]], axis=1))
            hi, lo = split(jnp.concatenate(parts, axis=0))
            chi[q] = right_dot(hi, lo, left[q])
        for u in range(2):
            waves(2 * jnp.minimum(j + 1, pairs - 1) + u, u)
        return carry

    for u in range(2):
        waves(u, u)
    lax.fori_loop(0, pairs, visit, jnp.int32(0))
    for u in range(2):
        deposit(2 * pairs - 2 + u, u)


def gather(positions, stage, grad, cols, rows):
    def part(i, carry):
        start = pl.multiple_of(i * 64, 64)
        for p in range(2):
            for b in cols:
                x = jnp.zeros((64, 128), F32)
                for k in range(stage.shape[2] // 512):
                    r, c = corner(positions, k)
                    x = x + stage[p, lax.rem(b + 1 - lax.div(c, 128), 4), pl.ds(512 * k + 256 + start - r, 64), :]
                grad[p, b, pl.ds(start, 64), :] = x
        return carry

    lax.fori_loop(rows.start // 64, rows.stop // 64, part, jnp.int32(0))


def sibling():
    gy, gx = lax.axis_index("gy"), lax.axis_index("gx")
    return gy, gx + 1 - 2 * lax.rem(gx, 2)


def along_x(d):
    gy, gx = lax.axis_index("gy"), lax.axis_index("gx")
    x = lax.div(gx, 4)
    return gy, lax.rem(x + d, 4) * 4 + lax.rem(gx, 4)


def member(j):
    gx = lax.axis_index("gx")
    place = lax.rem(j, 8)
    return lax.div(j, 8) * 4 + lax.div(place, 2), lax.div(gx, 4) * 4 + lax.rem(place, 2) * 2 + lax.rem(gx, 2)


class Sum:
    def __init__(self, total, full, acc0, acc1, acc2, rb0, rb1, rb2, send, recv):
        self.total, self.full, self.acc0, self.acc1, self.acc2 = total, full, acc0, acc1, acc2
        self.rb0, self.rb1, self.rb2 = rb0, rb1, rb2
        self.send, self.recv = send, recv
        gy, gx = lax.axis_index("gy"), lax.axis_index("gx")
        self.core, self.x = lax.rem(gx, 2), lax.div(gx, 4)
        self.mine = lax.rem(gy, 4) * 2 + lax.div(lax.rem(gx, 4), 2)
        self.me = lax.div(gy, 4) * 8 + self.mine
        self.tiles = total.shape[0] // 2

    def greet(self, barrier):
        devices = [sibling()] + [along_x(d) for d in (1, 2, 3)] + [member(lax.rem(self.me + d, 16)) for d in range(1, 16)]
        for device in devices:
            pl.semaphore_signal(barrier, inc=1, device_id=device, device_id_type=MESH)
        return len(devices)

    def copy(self, source, target, i, device):
        return pltpu.make_async_remote_copy(
            source, target, self.send.at[i], self.recv.at[i], device_id=device, device_id_type=MESH
        )

    def copies0(self):
        theirs = pl.ds(pl.multiple_of((1 - self.core) * 128, 128), 128)
        return [self.copy(self.total.at[:, theirs, :], self.rb0, 0, sibling())]

    def copies1(self):
        out = []
        for d in (1, 2, 3):
            part = pl.ds(pl.multiple_of(lax.rem(self.x + d, 4) * 32, 32), 32)
            out.append(self.copy(self.acc0.at[:, part, :], self.rb1.at[d - 1], d, along_x(d)))
        return out

    def copies2(self):
        out = []
        for d in range(1, 16):
            to = lax.rem(self.me + d, 16)
            part = pl.ds(lax.rem(to, 8) * self.tiles, self.tiles)
            out.append(self.copy(self.acc1.at[part], self.rb2.at[self.me], 3 + d, member(to)))
        return out

    def copies3(self):
        place = self.full.at[self.core, self.x, pl.ds(self.mine * self.tiles, self.tiles)]
        out = []
        for d in range(1, 8):
            to = lax.rem(self.mine + d, 8) + lax.div(self.me, 8) * 8
            out.append(self.copy(self.acc2, place, 18 + d, member(to)))
        return out

    def copies4(self):
        place = self.full.at[self.core, self.x]
        return [self.copy(place, place, 25 + d, along_x(d)) for d in (1, 2, 3)]

    def copies5(self):
        place = self.full.at[self.core]
        return [self.copy(place, place, 29, sibling())]

    def step(self, number):
        if number > 0:
            for c in getattr(self, f"copies{number - 1}")():
                c.wait_recv()
        if number == 1:
            own = pl.ds(pl.multiple_of(self.core * 128, 128), 128)
            self.acc0[...] = self.total[:, own, :] + self.rb0[...]
        if number == 2:
            own = pl.ds(pl.multiple_of(self.x * 32, 32), 32)
            x = self.acc0[:, own, :] + self.rb1[0] + self.rb1[1] + self.rb1[2]
            self.acc1[...] = x.reshape(self.acc1.shape)
            self.rb2[pl.ds(self.me, 1)] = self.acc1[pl.ds(self.mine * self.tiles, self.tiles)][None]
        if number == 3:
            x = self.rb2[0]
            for j in range(1, 16):
                x = x + self.rb2[j]
            self.acc2[...] = x
            self.full[pl.ds(self.core, 1), pl.ds(self.x, 1), pl.ds(self.mine * self.tiles, self.tiles)] = x[None, None]
        if number < 6:
            for c in getattr(self, f"copies{number}")():
                c.start()
        else:
            for stage in range(6):
                for c in getattr(self, f"copies{stage}")():
                    c.wait_send()


def sum_scratch(n):
    return [
        pltpu.VMEM((2, 4, 4 * n, 8, 128), F32),
        pltpu.VMEM((n, 128, 128), F32),
        pltpu.VMEM((4 * n, 8, 128), F32),
        pltpu.VMEM((n // 2, 8, 128), F32),
        pltpu.VMEM((n, 128, 128), F32),
        pltpu.VMEM((3, n, 32, 128), F32),
        pltpu.VMEM((16, n // 2, 8, 128), F32),
        pltpu.SemaphoreType.DMA((30,)),
        pltpu.SemaphoreType.DMA((30,)),
    ]


def new_probe(probe, full, write):
    parts = [full[h, x, 16:24] for h in range(2) for x in range(4)]
    top = parts[0]
    for w in parts[1:]:
        top = jnp.maximum(top, w)
    floor = 0.1 * jnp.max(top)
    for h in range(2):
        for x in range(4):
            rows = slice(128 * h + 32 * x, 128 * h + 32 * x + 32)
            for b in range(2):
                w = 0.9 * full[h, x, 16 + 4 * b : 20 + 4 * b].reshape(32, 128) + floor
                for p in range(2):
                    g = full[h, x, 8 * p + 4 * b : 8 * p + 4 * b + 4].reshape(32, 128)
                    write(p, b, rows, probe[p, b, rows, :] + g / w)


ORDERS = (
    ("s0", "gy", "s1", "y", "gx", "go", "s2", "x", "s3", "d", "s4", "w", "u", "cy", "s5", "cx", "cd", "s6", "p", "cw"),
    ("s0", "gy", "s1", "y", "gx", "go", "s2", "x", "s3", "d", "s4", "w", "u", "s5", "s6", "p"),
)


def kernel(positions, obj, probe, amps, right, left, sort, obj_out, probe_out, *refs):
    ext, grad, total, acc, probes, arranged, cut, lhs_hi, lhs_lo, chi, stage, inbox, send, recv, *rest = refs
    size = len(rest) // 2
    sums = [Sum(total, *rest[size * step : size * (step + 1)]) for step in range(2)]
    for step in range(2):
        blank_outside(ext.at[step])
    barrier, count = greet_sides()
    count = count + sums[0].greet(barrier)
    for b in range(2):
        lanes = slice(128 * b, 128 * b + 128)
        ext[0, :, 1 + b, 128:384, :] = obj[:, :, lanes]
        probes[0, :, b] = probe[:, :, lanes]

    def clear(k, carry):
        for p in range(2):
            for b in range(4):
                stage[p, b, pl.ds(pl.multiple_of(512 * k, 512), 256), :] = jnp.zeros((256, 128), F32)
            stage[p, 0, pl.ds(pl.multiple_of(512 * k + 256, 256), 256), :] = jnp.zeros((256, 128), F32)
        return carry

    lax.fori_loop(0, cut.shape[0], clear, jnp.int32(0))
    stage[:, :, 512 * cut.shape[0] :, :] = jnp.zeros((2, 4, 256, 128), F32)
    pl.semaphore_wait(barrier, count)
    copies = side_copies(ext.at[0], ext.at[0], True, send.at[0], recv.at[0])
    start_sides(copies)
    arrange(amps, sort, arranged)
    wait_sides(copies)
    for step in range(2):
        old, now = ext.at[step], probes.at[step]
        cut_patches(positions, old, cut, total)
        gradients(positions, cut, now, arranged, right, left, total, lhs_hi, lhs_lo, chi, stage)
        update(step, positions, stage, grad, inbox.at[step], acc, old, ext.at[1], now, probes.at[1], sums[step], send, recv, obj_out, probe_out)


def update(step, positions, stage, grad, inbox, acc, old, new, now, later, adder, send, recv, obj_out, probe_out):
    peak = jnp.max(now[0] * now[0] + now[1] * now[1])
    inward = side_copies(grad, inbox, False, send.at[1 + 2 * step], recv.at[1 + 2 * step])
    outward = side_copies(new, new, True, send.at[2], recv.at[2])

    def some(copies, kind):
        return [c for c, (dy, dx) in zip(copies, DIRS) if kind == ("d" if dy and dx else "y" if dy else "x")]

    def write(p, b, rows, x):
        if step == 1:
            probe_out[p, rows, 128 * b : 128 * b + 128] = x
        else:
            later[p, b, rows, :] = x

    for event in ORDERS[step]:
        if event == "gy":
            gather(positions, stage, grad, range(4), slice(0, 128))
            gather(positions, stage, grad, range(4), slice(384, 512))
        elif event == "gx":
            gather(positions, stage, grad, (0, 3), slice(128, 384))
        elif event == "go":
            gather(positions, stage, grad, (1, 2), slice(128, 384))
            acc[...] = grad[:, 1:3, 128:384, :]
        elif event in ("y", "x", "d"):
            start_sides(some(inward, event))
        elif event in ("cy", "cx", "cd"):
            start_sides(some(outward, event[1]))
        elif event == "cw":
            wait_sides(outward)
        elif event[0] == "s":
            adder.step(int(event[1]))
        elif event == "w":
            wait_sides(inward)
            for dy, dx in DIRS:
                cols, rows = halo_region(dy, dx)
                tcols, trows = edge_region(-dy, -dx)

                @pl.when(neighbor(-dy, -dx)[0])
                def _(cols=cols, rows=rows, tcols=tcols, trows=trows):
                    place = (slice(None), slice(tcols.start - 1, tcols.stop - 1), slice(trows.start - 128, trows.stop - 128))
                    acc[place] += inbox[:, cols, rows, :]

        elif event == "u" and step == 1:
            for b in range(2):
                obj_out[:, :, 128 * b : 128 * b + 128] = old[:, 1 + b, 128:384, :] + acc[:, b] / peak
        elif event == "u":
            new[:, 1:3, 128:384, :] = old[:, 1:3, 128:384, :] + acc[...] / peak
        else:
            new_probe(now, adder.full, write)


def shards(obj, probe, positions, amps):
    count = positions.shape[2]
    right, left = (jnp.asarray(t) for t in tables())
    tile = jax.ShapeDtypeStruct((2, 256, 256), F32)
    ext = (2, 4, 512, 128)
    return pl.pallas_call(
        kernel,
        out_shape=(tile, tile),
        in_specs=[SMEM] + [VMEM] * 6,
        out_specs=(VMEM, VMEM),
        scratch_shapes=[
            pltpu.VMEM((2, *ext), F32),
            pltpu.VMEM(ext, F32),
            pltpu.VMEM((6, 256, 128), F32),
            pltpu.VMEM((2, 2, 256, 128), F32),
            pltpu.VMEM((2, 2, 2, 256, 128), F32),
            pltpu.VMEM((count, 256, 256), BF16),
            pltpu.VMEM((count, 2, 2, 256, 128), F32),
            pltpu.VMEM((2, 512, 256), BF16),
            pltpu.VMEM((2, 512, 256), BF16),
            pltpu.VMEM((2, 512, 256), F32),
            pltpu.VMEM((2, 4, 512 * count + 256, 128), F32),
            pltpu.VMEM((2, *ext), F32),
            pltpu.SemaphoreType.DMA((4, 8)),
            pltpu.SemaphoreType.DMA((4, 8)),
            *sum_scratch(6) * 2,
        ],
        compiler_params=pltpu.CompilerParams(collective_id=0, has_side_effects=True, vmem_limit_bytes=VMEM_LIMIT),
        name="iterations",
    )(positions, obj, probe, amps, right, left, jnp.asarray(sorting()))


def solution(mesh):
    in_specs = (
        P(None, "gy", "gx"),
        P(),
        P("gy", "gx", None, None),
        P("gy", "gx", None, None, None),
    )
    out_specs = (P(None, "gy", "gx"), P())
    return jax.shard_map(shards, mesh=mesh, in_specs=in_specs, out_specs=out_specs, check_vma=False)
```

time: 153 us -> 140 us (0.915)
  Pallas kernels: 148 us -> 135 us
    pallas_call x1, Pallas kernels: 148 us -> 135 us  [shards(): pl.pallas_call(kernel, out_shape=(tile, tile), in_specs=[SMEM] + [VMEM] *...]
where the time goes in v3:
time: 140 us
  Pallas kernels  135 us (96%)
  local copies, waits for them, and re-layouts  4.07 us (3%)
    pallas_call x1, Pallas kernels, shards(): pl.pallas_call(kernel, out_shape=(tile, tile), in_specs=[SMEM] + [VMEM] *...  135 us
    unnamed x5, local copies, waits for them, and re-layouts  4.07 us

profile of v3, /device:TPU:1, one launch (start us, length us, event | category | flops | bytes accessed | tf_op | source)
XLA Modules:
  0.0 140.0 jit_solution(9035918096472182814)
XLA Ops:
  0.6 1.3 copy.9.positions
  2.0 135.3 %iterations.1 = (f32[2,256,256]{2,1,0:T(8,128)}, f32[2,256,256]{2,1,0:T(8,128)}) custom-call(s32[1,1,8,2]{3,2,1,0:T(8,128)} %copy.9.positions, f32[2,256,256]{2,1,0:T(8,128)} %obj.1, f32[2,256,256]{2,1,0:T(8,128)} %probe.1, bf16[1,1,8,256,256]{4,3,2,1,0:T(8,128)(2,1)} %amps.1, bf16[2,2,256,256]{3,2,1,0:T(8,128)(2,1)} %constant.6.clone.right, ...), custom_call_target="tpu_custom_call" | custom-call | tf_op jit(solution)/shard_map/iterations/pallas_call | solution.py:516
  137.2 0.0 copy-start
  137.3 1.9 %copy.12 = f32[2,256,256]{2,1,0:T(8,128)} copy(f32[2,256,256]{2,1,0:T(8,128)} %get-tuple-element.4) | data formatting | bytes 1048576
  139.2 0.0 copy-done
  139.2 0.8 copy.13
Async XLA Ops:
  137.2 1.9 %copy-start = (f32[2,256,256]{2,1,0:T(8,128)S(1)}, f32[2,256,256]{2,1,0:T(8,128)}, u32[]{:S(2)}) copy-start(f32[2,256,256]{2,1,0:T(8,128)} %get-tuple-element.5) | copy-start | bytes 1572868

commit v4 on v3

--- a/solution.py
+++ b/solution.py
@@ -16,7 +16,8 @@
 SMEM = pl.BlockSpec(memory_space=pltpu.SMEM)
 VMEM_LIMIT = 60 * 1024 * 1024
 
-DIRS = [(-1, 0), (1, 0), (0, -1), (0, 1), (-1, -1), (-1, 1), (1, -1), (1, 1)]
+TOP, UPPER, LOWER, BOTTOM = (slice(128 * i, 128 * i + 128) for i in range(4))
+MIDDLE = slice(128, 384)
 
 
 def tables():
@@ -40,31 +41,29 @@
     return np.stack([m, m.T]).astype(ml_dtypes.bfloat16)
 
 
-def neighbor(dy, dx):
-    y = lax.axis_index("gy") + dy
-    x = lax.axis_index("gx") + dx
+def around():
+    gy, gx = lax.axis_index("gy"), lax.axis_index("gx")
+    core = lax.rem(gx, 2)
+    outer = jnp.where(core == 0, gx > 0, gx < lax.axis_size("gx") - 1)
+    return core, gy > 0, gy < lax.axis_size("gy") - 1, outer
+
+
+def devices_around():
+    gy, gx = lax.axis_index("gy"), lax.axis_index("gx")
+    core = lax.rem(gx, 2)
     ny, nx = lax.axis_size("gy"), lax.axis_size("gx")
-    ok = (y >= 0) & (y < ny) & (x >= 0) & (x < nx)
-    return ok, (jnp.clip(y, 0, ny - 1), jnp.clip(x, 0, nx - 1))
-
-
-def halo_region(dy, dx):
-    rows = {-1: slice(0, 128), 0: slice(128, 384), 1: slice(384, 512)}[dy]
-    cols = {-1: slice(0, 1), 0: slice(1, 3), 1: slice(3, 4)}[dx]
-    return cols, rows
-
-
-def edge_region(dy, dx):
-    rows = {-1: slice(128, 256), 0: slice(128, 384), 1: slice(256, 384)}[dy]
-    cols = {-1: slice(1, 2), 0: slice(1, 3), 1: slice(2, 3)}[dx]
-    return cols, rows
+    return (
+        (jnp.maximum(gy - 1, 0), gx),
+        (jnp.minimum(gy + 1, ny - 1), gx),
+        (gy, jnp.clip(gx + 2 * core - 1, 0, nx - 1)),
+        (gy, gx + 1 - 2 * core),
+    )
 
 
 def greet_sides():
     barrier = pltpu.get_barrier_semaphore()
     count = jnp.int32(0)
-    for d in DIRS:
-        ok, device = neighbor(*d)
+    for ok, device in zip(around()[1:], devices_around()):
 
         @pl.when(ok)
         def _(device=device):
@@ -74,27 +73,74 @@
     return barrier, count
 
 
-def side_copies(source, target, outward, send, recv):
-    out = []
-    for i, (dy, dx) in enumerate(DIRS):
-        ok, device = neighbor(dy, dx)
-        cols, rows = edge_region(dy, dx) if outward else halo_region(dy, dx)
-        tcols, trows = halo_region(-dy, -dx) if outward else (cols, rows)
-        out.append(
-            (
-                ok,
-                neighbor(-dy, -dx)[0],
-                pltpu.make_async_remote_copy(
-                    source.at[:, cols, rows, :],
-                    target.at[:, tcols, trows, :],
-                    send.at[i],
-                    recv.at[i],
-                    device_id=device,
-                    device_id_type=MESH,
-                ),
-            )
+def sides(send, recv):
+    slots = iter(range(16))
+
+    def link(goes, comes, source, target, device):
+        i = next(slots)
+        return (
+            goes,
+            comes,
+            pltpu.make_async_remote_copy(
+                source, target, send.at[i], recv.at[i], device_id=device, device_id_type=MESH
+            ),
         )
-    return out
+
+    return link
+
+
+def outward(ext, send, recv):
+    core, up, down, outer = around()
+    above, below, beside, other = devices_around()
+    link = sides(send, recv)
+    edge, inner = pl.ds(1 + core, 1), pl.ds(2 - core, 1)
+    halo, far = pl.ds(3 * core, 1), pl.ds(3 - 3 * core, 1)
+    always = up | jnp.logical_not(up)
+    return {
+        "y": [
+            link(up, down, ext.at[:, 1:3, UPPER], ext.at[:, 1:3, BOTTOM], above),
+            link(down, up, ext.at[:, 1:3, LOWER], ext.at[:, 1:3, TOP], below),
+        ],
+        "x": [link(outer, outer, ext.at[:, edge, MIDDLE], ext.at[:, far, MIDDLE], beside)],
+        "i": [link(always, always, ext.at[:, inner, MIDDLE], ext.at[:, halo, MIDDLE], other)],
+        "xy": [
+            link(up & outer, down & outer, ext.at[:, halo, UPPER], ext.at[:, halo, BOTTOM], above),
+            link(down & outer, up & outer, ext.at[:, halo, LOWER], ext.at[:, halo, TOP], below),
+        ],
+        "iy": [
+            link(up, up, ext.at[:, inner, TOP], ext.at[:, halo, TOP], other),
+            link(down, down, ext.at[:, inner, BOTTOM], ext.at[:, halo, BOTTOM], other),
+        ],
+    }
+
+
+def inward(grad, box, corners, send, recv):
+    core, up, down, outer = around()
+    above, below, beside, other = devices_around()
+    link = sides(send, recv)
+    edge, inner = pl.ds(1 + core, 1), pl.ds(2 - core, 1)
+    halo, far = pl.ds(3 * core, 1), pl.ds(3 - 3 * core, 1)
+    always = up | jnp.logical_not(up)
+    return {
+        "xy": [
+            link(up & outer, down & outer, grad.at[:, halo, TOP], corners.at[:, 0:1], above),
+            link(down & outer, up & outer, grad.at[:, halo, BOTTOM], corners.at[:, 1:2], below),
+        ],
+        "iy": [
+            link(up, up, grad.at[:, far, TOP], corners.at[:, 2:3], other),
+            link(down, down, grad.at[:, far, BOTTOM], corners.at[:, 3:4], other),
+        ],
+        "y": [
+            link(up, down, grad.at[:, edge, TOP], box.at[:, edge, TOP], above),
+            link(down, up, grad.at[:, edge, BOTTOM], box.at[:, edge, BOTTOM], below),
+        ],
+        "z": [
+            link(up, down, grad.at[:, inner, TOP], box.at[:, inner, TOP], above),
+            link(down, up, grad.at[:, inner, BOTTOM], box.at[:, inner, BOTTOM], below),
+        ],
+        "i": [link(always, always, grad.at[:, far, MIDDLE], box.at[:, far, MIDDLE], other)],
+        "x": [link(outer, outer, grad.at[:, halo, MIDDLE], box.at[:, halo, MIDDLE], beside)],
+    }
 
 
 def start_sides(copies):
@@ -102,18 +148,28 @@
         pl.when(ok)(copy.start)
 
 
-def wait_sides(copies):
-    for ok, arrives, copy in copies:
+def take_sides(copies):
+    for _, arrives, copy in copies:
+        pl.when(arrives)(copy.wait_recv)
+
+
+def leave_sides(copies):
+    for ok, _, copy in copies:
         pl.when(ok)(copy.wait_send)
-        pl.when(arrives)(copy.wait_recv)
 
 
 def blank_outside(ext):
-    for dy, dx in DIRS:
-        cols, rows = halo_region(dy, dx)
-
-        @pl.when(jnp.logical_not(neighbor(dy, dx)[0]))
-        def _(cols=cols, rows=rows):
+    gy, gx = lax.axis_index("gy"), lax.axis_index("gx")
+    for outside, place in (
+        (gy == 0, (slice(0, 4), TOP)),
+        (gy == lax.axis_size("gy") - 1, (slice(0, 4), BOTTOM)),
+        (gx == 0, (slice(0, 1), slice(0, 512))),
+        (gx == lax.axis_size("gx") - 1, (slice(3, 4), slice(0, 512))),
+    ):
+
+        @pl.when(outside)
+        def _(place=place):
+            cols, rows = place
             ext[:, cols, rows, :] = jnp.zeros((2, cols.stop - cols.start, rows.stop - rows.start, 128), F32)
 
 
@@ -418,13 +474,13 @@
 
 
 ORDERS = (
-    ("s0", "gy", "s1", "y", "gx", "go", "s2", "x", "s3", "d", "s4", "w", "u", "cy", "s5", "cx", "cd", "s6", "p", "cw"),
-    ("s0", "gy", "s1", "y", "gx", "go", "s2", "x", "s3", "d", "s4", "w", "u", "s5", "s6", "p"),
+    ("s0", "gh", "b0", "s1", "go", "b1", "b2", "s2", "s3", "s4", "w", "u", "c0", "s5", "c1", "c2", "s6", "p", "cw"),
+    ("s0", "gh", "b0", "s1", "go", "b1", "s2", "b2", "s3", "s4", "w", "u", "s5", "s6", "p"),
 )
 
 
 def kernel(positions, obj, probe, amps, right, left, sort, obj_out, probe_out, *refs):
-    ext, grad, total, acc, probes, arranged, cut, lhs_hi, lhs_lo, chi, stage, inbox, send, recv, *rest = refs
+    ext, grad, total, acc, probes, arranged, cut, lhs_hi, lhs_lo, chi, stage, inbox, corners, send, recv, *rest = refs
     size = len(rest) // 2
     sums = [Sum(total, *rest[size * step : size * (step + 1)]) for step in range(2)]
     for step in range(2):
@@ -446,24 +502,34 @@
     lax.fori_loop(0, cut.shape[0], clear, jnp.int32(0))
     stage[:, :, 512 * cut.shape[0] :, :] = jnp.zeros((2, 4, 256, 128), F32)
     pl.semaphore_wait(barrier, count)
-    copies = side_copies(ext.at[0], ext.at[0], True, send.at[0], recv.at[0])
-    start_sides(copies)
+    copies = outward(ext.at[0], send.at[0], recv.at[0])
+    start_sides(copies["x"] + copies["y"] + copies["i"])
+    take_sides(copies["x"])
+    start_sides(copies["xy"])
     arrange(amps, sort, arranged)
-    wait_sides(copies)
+    take_sides(copies["y"])
+    start_sides(copies["iy"])
+    take_sides(copies["xy"] + copies["i"] + copies["iy"])
+    leave_sides(sum(copies.values(), []))
     for step in range(2):
         old, now = ext.at[step], probes.at[step]
         cut_patches(positions, old, cut, total)
         gradients(positions, cut, now, arranged, right, left, total, lhs_hi, lhs_lo, chi, stage)
-        update(step, positions, stage, grad, inbox.at[step], acc, old, ext.at[1], now, probes.at[1], sums[step], send, recv, obj_out, probe_out)
-
-
-def update(step, positions, stage, grad, inbox, acc, old, new, now, later, adder, send, recv, obj_out, probe_out):
+        update(step, positions, stage, grad, inbox.at[step], corners.at[step], acc, old, ext.at[1], now, probes.at[1], sums[step], send, recv, obj_out, probe_out)
+
+
+def update(step, positions, stage, grad, inbox, corners, acc, old, new, now, later, adder, send, recv, obj_out, probe_out):
     peak = jnp.max(now[0] * now[0] + now[1] * now[1])
-    inward = side_copies(grad, inbox, False, send.at[1 + 2 * step], recv.at[1 + 2 * step])
-    outward = side_copies(new, new, True, send.at[2], recv.at[2])
-
-    def some(copies, kind):
-        return [c for c, (dy, dx) in zip(copies, DIRS) if kind == ("d" if dy and dx else "y" if dy else "x")]
+    into = inward(grad, inbox, corners, send.at[1 + 2 * step], recv.at[1 + 2 * step])
+    out = outward(new, send.at[2], recv.at[2]) if step == 0 else None
+    core, up, down, outer = around()
+    gx = lax.axis_index("gx")
+    inner, halo = pl.ds(2 - core, 1), pl.ds(3 * core, 1)
+
+    def add(where, target, place, value):
+        @pl.when(where)
+        def _():
+            target[place] += value()
 
     def write(p, b, rows, x):
         if step == 1:
@@ -472,33 +538,46 @@
             later[p, b, rows, :] = x
 
     for event in ORDERS[step]:
-        if event == "gy":
-            gather(positions, stage, grad, range(4), slice(0, 128))
-            gather(positions, stage, grad, range(4), slice(384, 512))
-        elif event == "gx":
-            gather(positions, stage, grad, (0, 3), slice(128, 384))
+        if event == "gh":
+            gather(positions, stage, grad, range(4), TOP)
+            gather(positions, stage, grad, range(4), BOTTOM)
+            gather(positions, stage, grad, (0, 3), MIDDLE)
         elif event == "go":
-            gather(positions, stage, grad, (1, 2), slice(128, 384))
-            acc[...] = grad[:, 1:3, 128:384, :]
-        elif event in ("y", "x", "d"):
-            start_sides(some(inward, event))
-        elif event in ("cy", "cx", "cd"):
-            start_sides(some(outward, event[1]))
+            gather(positions, stage, grad, (1, 2), MIDDLE)
+            acc[...] = grad[:, 1:3, MIDDLE, :]
+        elif event == "b0":
+            start_sides(into["iy"] + into["xy"] + into["y"] + into["i"])
+        elif event == "b1":
+            take_sides(into["iy"])
+            add(up, grad, (slice(None), inner, TOP), lambda: corners[:, 2:3])
+            add(down, grad, (slice(None), inner, BOTTOM), lambda: corners[:, 3:4])
+            start_sides(into["z"])
+        elif event == "b2":
+            take_sides(into["xy"])
+            add(down & outer, grad, (slice(None), halo, LOWER), lambda: corners[:, 0:1])
+            add(up & outer, grad, (slice(None), halo, UPPER), lambda: corners[:, 1:2])
+            start_sides(into["x"])
+        elif event == "w":
+            take_sides(into["y"] + into["z"] + into["i"] + into["x"])
+            leave_sides(sum(into.values(), []))
+            every = slice(None)
+            add(down, acc, (every, every, slice(128, 256)), lambda: inbox[:, 1:3, TOP])
+            add(up, acc, (every, every, slice(0, 128)), lambda: inbox[:, 1:3, BOTTOM])
+            add(gx > 0, acc, (every, 0), lambda: inbox[:, 3, MIDDLE])
+            add(gx < lax.axis_size("gx") - 1, acc, (every, 1), lambda: inbox[:, 0, MIDDLE])
+        elif event == "c0":
+            start_sides(out["x"] + out["y"] + out["i"])
+        elif event == "c1":
+            take_sides(out["x"])
+            start_sides(out["xy"])
+        elif event == "c2":
+            take_sides(out["y"])
+            start_sides(out["iy"])
         elif event == "cw":
-            wait_sides(outward)
+            take_sides(out["xy"] + out["i"] + out["iy"])
+            leave_sides(sum(out.values(), []))
         elif event[0] == "s":
             adder.step(int(event[1]))
-        elif event == "w":
-            wait_sides(inward)
-            for dy, dx in DIRS:
-                cols, rows = halo_region(dy, dx)
-                tcols, trows = edge_region(-dy, -dx)
-
-                @pl.when(neighbor(-dy, -dx)[0])
-                def _(cols=cols, rows=rows, tcols=tcols, trows=trows):
-                    place = (slice(None), slice(tcols.start - 1, tcols.stop - 1), slice(trows.start - 128, trows.stop - 128))
-                    acc[place] += inbox[:, cols, rows, :]
-
         elif event == "u" and step == 1:
             for b in range(2):
                 obj_out[:, :, 128 * b : 128 * b + 128] = old[:, 1 + b, 128:384, :] + acc[:, b] / peak
@@ -531,8 +610,9 @@
             pltpu.VMEM((2, 512, 256), F32),
             pltpu.VMEM((2, 4, 512 * count + 256, 128), F32),
             pltpu.VMEM((2, *ext), F32),
-            pltpu.SemaphoreType.DMA((4, 8)),
-            pltpu.SemaphoreType.DMA((4, 8)),
+            pltpu.VMEM((2, 2, 4, 128, 128), F32),
+            pltpu.SemaphoreType.DMA((4, 16)),
+            pltpu.SemaphoreType.DMA((4, 16)),
             *sum_scratch(6) * 2,
         ],
         compiler_params=pltpu.CompilerParams(collective_id=0, has_side_effects=True, vmem_limit_bytes=VMEM_LIMIT),

time: 140 us -> 131 us (0.936)
  Pallas kernels: 135 us -> 126 us
    pallas_call x1, Pallas kernels: 135 us -> 126 us  [shards(): pl.pallas_call(kernel, out_shape=(tile, tile), in_specs=[SMEM] + [VMEM] *...]
where the time goes in v4:
time: 131 us; the launch traced here: 130 us
  Pallas kernels  126 us (96%)
  local copies, waits for them, and re-layouts  4.07 us (3%)
    pallas_call x1, Pallas kernels, shards(): pl.pallas_call(kernel, out_shape=(tile, tile), in_specs=[SMEM] + [VMEM] *...  126 us
    unnamed x5, local copies, waits for them, and re-layouts  4.07 us

profile of v4, /device:TPU:1, one launch (start us, length us, event | category | flops | bytes accessed | tf_op | source)
XLA Modules:
  0.0 130.5 jit_solution(14813799659661221386)
XLA Ops:
  0.6 1.3 %copy.9.positions = s32[1,1,8,2]{3,2,1,0:T(8,128)} copy(s32[1,1,8,2]{2,3,1,0:T(2,128)} %param.9) | data formatting | bytes 128 | tf_op args[2]
  2.0 125.8 %iterations.1 = (f32[2,256,256]{2,1,0:T(8,128)}, f32[2,256,256]{2,1,0:T(8,128)}) custom-call(s32[1,1,8,2]{3,2,1,0:T(8,128)} %copy.9.positions, f32[2,256,256]{2,1,0:T(8,128)} %obj.1, f32[2,256,256]{2,1,0:T(8,128)} %probe.1, bf16[1,1,8,256,256]{4,3,2,1,0:T(8,128)(2,1)} %amps.1, bf16[2,2,256,256]{3,2,1,0:T(8,128)(2,1)} %constant.6.clone.right, ...), custom_call_target="tpu_custom_call" | custom-call | tf_op jit(solution)/shard_map/iterations/pallas_call | solution.py:595
  127.7 0.0 copy-start
  127.8 1.9 %copy.12 = f32[2,256,256]{2,1,0:T(8,128)} copy(f32[2,256,256]{2,1,0:T(8,128)} %get-tuple-element.4) | data formatting | bytes 1048576
  129.7 0.0 copy-done
  129.7 0.8 copy.13
Async XLA Ops:
  127.7 1.9 %copy-start = (f32[2,256,256]{2,1,0:T(8,128)S(1)}, f32[2,256,256]{2,1,0:T(8,128)}, u32[]{:S(2)}) copy-start(f32[2,256,256]{2,1,0:T(8,128)} %get-tuple-element.5) | copy-start | bytes 1572868

commit v5 on v4

--- a/solution.py
+++ b/solution.py
@@ -175,7 +175,7 @@
 
 def arrange(amps, sort, out):
     def one(k, carry):
-        half = jnp.dot(sort[0], amps[0, 0, k], preferred_element_type=F32).astype(BF16)
+        half = jnp.dot(sort[0], amps[k], preferred_element_type=F32).astype(BF16)
         out[k] = jnp.dot(half, sort[1], preferred_element_type=F32).astype(BF16)
         return carry
 
@@ -196,11 +196,8 @@
 
 
 def left_dot(m, hi, lo):
-    return jnp.dot(
-        jnp.concatenate([m[0], m[0], m[1]], axis=1),
-        jnp.concatenate([hi, lo, hi], axis=0),
-        preferred_element_type=F32,
-    )
+    first = jnp.dot(jnp.concatenate([m[0], m[1]], axis=0), hi, preferred_element_type=F32)
+    return first[:256] + (first[256:] + jnp.dot(m[0], lo, preferred_element_type=F32))
 
 
 def corner(positions, k):
@@ -235,7 +232,7 @@
     lax.fori_loop(0, cut.shape[0], visit, jnp.int32(0))
 
 
-def gradients(positions, cut, probe, amps, right, left, total, lhs_hi, lhs_lo, chi, stage):
+def gradients(positions, cut, probe, amps, right, left, total, lhs_hi, lhs_lo, chi, stage, heavy):
     total[0:4] = jnp.zeros((4, 256, 128), F32)
     chi[...] = jnp.zeros_like(chi)
     lane = lax.broadcasted_iota(jnp.int32, (1, 128), 1)
@@ -300,6 +297,8 @@
         return out
 
     def visit(j, carry):
+        pl.when(j == 1)(functools.partial(heavy.step, 1))
+        pl.when(j == pairs - 1)(functools.partial(heavy.step, 2))
         y = [right_dot(lhs_hi[q], lhs_lo[q], right[q]) for q in range(2)]
         for u in range(2):
             deposit(2 * jnp.maximum(j - 1, 0) + u, u)
@@ -457,8 +456,8 @@
     ]
 
 
-def new_probe(probe, full, write):
-    parts = [full[h, x, 16:24] for h in range(2) for x in range(4)]
+def new_probe(probe, full, weight, write):
+    parts = [weight[h, x] for h in range(2) for x in range(4)]
     top = parts[0]
     for w in parts[1:]:
         top = jnp.maximum(top, w)
@@ -467,22 +466,32 @@
         for x in range(4):
             rows = slice(128 * h + 32 * x, 128 * h + 32 * x + 32)
             for b in range(2):
-                w = 0.9 * full[h, x, 16 + 4 * b : 20 + 4 * b].reshape(32, 128) + floor
+                w = 0.9 * weight[h, x, 4 * b : 4 * b + 4].reshape(32, 128) + floor
                 for p in range(2):
                     g = full[h, x, 8 * p + 4 * b : 8 * p + 4 * b + 4].reshape(32, 128)
                     write(p, b, rows, probe[p, b, rows, :] + g / w)
 
 
 ORDERS = (
-    ("s0", "gh", "b0", "s1", "go", "b1", "b2", "s2", "s3", "s4", "w", "u", "c0", "s5", "c1", "c2", "s6", "p", "cw"),
-    ("s0", "gh", "b0", "s1", "go", "b1", "s2", "b2", "s3", "s4", "w", "u", "s5", "s6", "p"),
+    ("s0", "g0", "s1", "g1", "g2", "t3", "go", "b1", "b2", "s2", "t4", "s3", "s4", "t5", "w", "u", "c0", "s5", "c1", "c2", "s6", "t6", "p", "cw"),
+    ("s0", "g0", "s1", "g1", "g2", "t3", "go", "s2", "b1", "b2", "t4", "s3", "t5", "s4", "w", "u", "s5", "s6", "t6", "p"),
 )
 
 
-def kernel(positions, obj, probe, amps, right, left, sort, obj_out, probe_out, *refs):
-    ext, grad, total, acc, probes, arranged, cut, lhs_hi, lhs_lo, chi, stage, inbox, corners, send, recv, *rest = refs
-    size = len(rest) // 2
-    sums = [Sum(total, *rest[size * step : size * (step + 1)]) for step in range(2)]
+def kernel(positions, obj, probe, amps_far, right_far, left_far, sort_far, obj_out, probe_out, *refs):
+    amps, right, left, sort, load, ext, grad, total, acc, probes, arranged, cut, lhs_hi, lhs_lo, chi, stage, inbox, corners, send, recv, *rest = refs
+    size = len(rest) // 4
+    parts = [rest[size * i : size * (i + 1)] for i in range(4)]
+    sums = [Sum(total.at[0:4], *parts[step]) for step in range(2)]
+    weights = [Sum(total.at[4:6], *parts[2 + step]) for step in range(2)]
+    loads = [
+        pltpu.make_async_copy(source, target, load.at[i])
+        for i, (source, target) in enumerate(
+            ((amps_far.at[0, 0], amps), (sort_far, sort), (right_far, right), (left_far, left))
+        )
+    ]
+    for c in loads:
+        c.start()
     for step in range(2):
         blank_outside(ext.at[step])
     barrier, count = greet_sides()
@@ -506,6 +515,8 @@
     start_sides(copies["x"] + copies["y"] + copies["i"])
     take_sides(copies["x"])
     start_sides(copies["xy"])
+    for c in loads:
+        c.wait()
     arrange(amps, sort, arranged)
     take_sides(copies["y"])
     start_sides(copies["iy"])
@@ -514,11 +525,12 @@
     for step in range(2):
         old, now = ext.at[step], probes.at[step]
         cut_patches(positions, old, cut, total)
-        gradients(positions, cut, now, arranged, right, left, total, lhs_hi, lhs_lo, chi, stage)
-        update(step, positions, stage, grad, inbox.at[step], corners.at[step], acc, old, ext.at[1], now, probes.at[1], sums[step], send, recv, obj_out, probe_out)
-
-
-def update(step, positions, stage, grad, inbox, corners, acc, old, new, now, later, adder, send, recv, obj_out, probe_out):
+        weights[step].step(0)
+        gradients(positions, cut, now, arranged, right, left, total, lhs_hi, lhs_lo, chi, stage, weights[step])
+        update(step, positions, stage, grad, inbox.at[step], corners.at[step], acc, old, ext.at[1], now, probes.at[1], sums[step], weights[step], send, recv, obj_out, probe_out)
+
+
+def update(step, positions, stage, grad, inbox, corners, acc, old, new, now, later, adder, heavy, send, recv, obj_out, probe_out):
     peak = jnp.max(now[0] * now[0] + now[1] * now[1])
     into = inward(grad, inbox, corners, send.at[1 + 2 * step], recv.at[1 + 2 * step])
     out = outward(new, send.at[2], recv.at[2]) if step == 0 else None
@@ -538,15 +550,16 @@
             later[p, b, rows, :] = x
 
     for event in ORDERS[step]:
-        if event == "gh":
-            gather(positions, stage, grad, range(4), TOP)
-            gather(positions, stage, grad, range(4), BOTTOM)
+        if event in ("g0", "g1"):
+            i = int(event[1])
+            gather(positions, stage, grad, range(4), (TOP, BOTTOM)[i])
+            start_sides([into["xy"][i], into["iy"][i], into["y"][i]])
+        elif event == "g2":
             gather(positions, stage, grad, (0, 3), MIDDLE)
+            start_sides(into["i"])
         elif event == "go":
             gather(positions, stage, grad, (1, 2), MIDDLE)
             acc[...] = grad[:, 1:3, MIDDLE, :]
-        elif event == "b0":
-            start_sides(into["iy"] + into["xy"] + into["y"] + into["i"])
         elif event == "b1":
             take_sides(into["iy"])
             add(up, grad, (slice(None), inner, TOP), lambda: corners[:, 2:3])
@@ -578,13 +591,15 @@
             leave_sides(sum(out.values(), []))
         elif event[0] == "s":
             adder.step(int(event[1]))
+        elif event[0] == "t":
+            heavy.step(int(event[1]))
         elif event == "u" and step == 1:
             for b in range(2):
                 obj_out[:, :, 128 * b : 128 * b + 128] = old[:, 1 + b, 128:384, :] + acc[:, b] / peak
         elif event == "u":
             new[:, 1:3, 128:384, :] = old[:, 1:3, 128:384, :] + acc[...] / peak
         else:
-            new_probe(now, adder.full, write)
+            new_probe(now, adder.full, heavy.full, write)
 
 
 def shards(obj, probe, positions, amps):
@@ -592,12 +607,18 @@
     right, left = (jnp.asarray(t) for t in tables())
     tile = jax.ShapeDtypeStruct((2, 256, 256), F32)
     ext = (2, 4, 512, 128)
+    anywhere = pl.BlockSpec(memory_space=pl.ANY)
     return pl.pallas_call(
         kernel,
         out_shape=(tile, tile),
-        in_specs=[SMEM] + [VMEM] * 6,
+        in_specs=[SMEM] + [VMEM] * 2 + [anywhere] * 4,
         out_specs=(VMEM, VMEM),
         scratch_shapes=[
+            pltpu.VMEM((count, 256, 256), BF16),
+            pltpu.VMEM((2, 2, 256, 256), BF16),
+            pltpu.VMEM((2, 2, 256, 256), BF16),
+            pltpu.VMEM((2, 256, 256), BF16),
+            pltpu.SemaphoreType.DMA((4,)),
             pltpu.VMEM((2, *ext), F32),
             pltpu.VMEM(ext, F32),
             pltpu.VMEM((6, 256, 128), F32),
@@ -613,7 +634,8 @@
             pltpu.VMEM((2, 2, 4, 128, 128), F32),
             pltpu.SemaphoreType.DMA((4, 16)),
             pltpu.SemaphoreType.DMA((4, 16)),
-            *sum_scratch(6) * 2,
+            *sum_scratch(4) * 2,
+            *sum_scratch(2) * 2,
         ],
         compiler_params=pltpu.CompilerParams(collective_id=0, has_side_effects=True, vmem_limit_bytes=VMEM_LIMIT),
         name="iterations",

time: 131 us -> 127 us (0.969)
  Pallas kernels: 126 us -> 122 us
    pallas_call x1, Pallas kernels: 126 us -> 122 us  [shards(): pl.pallas_call(kernel, out_shape=(tile, tile), in_specs=[SMEM] + [VMEM] *...]
where the time goes in v5:
time: 127 us
  Pallas kernels  122 us (96%)
  local copies, waits for them, and re-layouts  4.07 us (3%)
    pallas_call x1, Pallas kernels, shards(): pl.pallas_call(kernel, out_shape=(tile, tile), in_specs=[SMEM] + [VMEM] *...  122 us
    unnamed x5, local copies, waits for them, and re-layouts  4.07 us

profile of v5, /device:TPU:1, one launch (start us, length us, event | category | flops | bytes accessed | tf_op | source)
XLA Modules:
  0.0 127.1 jit_solution(4242837534187248057)
XLA Ops:
  0.6 1.3 %copy.9.positions = s32[1,1,8,2]{3,2,1,0:T(8,128)} copy(s32[1,1,8,2]{2,3,1,0:T(2,128)} %param.9) | data formatting | bytes 128 | tf_op args[2]
  2.0 122.4 %iterations.1 = (f32[2,256,256]{2,1,0:T(8,128)}, f32[2,256,256]{2,1,0:T(8,128)}) custom-call(s32[1,1,8,2]{3,2,1,0:T(8,128)} %copy.9.positions, f32[2,256,256]{2,1,0:T(8,128)} %obj.1, f32[2,256,256]{2,1,0:T(8,128)} %probe.1, bf16[1,1,8,256,256]{4,3,2,1,0:T(8,128)(2,1)} %amps_far.1, bf16[2,2,256,256]{3,2,1,0:T(8,128)(2,1)} %constant.6.clone.right_far, ...), custom_call_target="tpu_custom_call" | custom-call | tf_op jit(solution)/shard_map/iterations/pallas_call | solution.py:611
  124.4 0.0 copy-start
  124.4 1.9 %copy.12 = f32[2,256,256]{2,1,0:T(8,128)} copy(f32[2,256,256]{2,1,0:T(8,128)} %get-tuple-element.4) | data formatting | bytes 1048576
  126.3 0.0 copy-done
  126.3 0.8 copy.13
Async XLA Ops:
  124.4 1.9 %copy-start = (f32[2,256,256]{2,1,0:T(8,128)S(1)}, f32[2,256,256]{2,1,0:T(8,128)}, u32[]{:S(2)}) copy-start(f32[2,256,256]{2,1,0:T(8,128)} %get-tuple-element.5) | copy-start | bytes 1572868

commit v6 on v5

--- a/solution.py
+++ b/solution.py
@@ -201,8 +201,8 @@
 
 
 def corner(positions, k):
-    row = positions[0, 0, k, 0] - lax.axis_index("gy") * 256 + 128
-    col = positions[0, 0, k, 1] - lax.axis_index("gx") * 256 + 128
+    row = positions[0, 0, 0, k] - lax.axis_index("gy") * 256 + 128
+    col = positions[0, 0, 1, k] - lax.axis_index("gx") * 256 + 128
     return jnp.clip(row, 0, 255), jnp.clip(col, 0, 255)
 
 
@@ -473,7 +473,7 @@
 
 
 ORDERS = (
-    ("s0", "g0", "s1", "g1", "g2", "t3", "go", "b1", "b2", "s2", "t4", "s3", "s4", "t5", "w", "u", "c0", "s5", "c1", "c2", "s6", "t6", "p", "cw"),
+    ("s0", "g0", "s1", "g1", "g2", "t3", "go", "s2", "b1", "b2", "t4", "s3", "t5", "s4", "w", "u", "c0", "s5", "c1", "c2", "s6", "t6", "p", "cw"),
     ("s0", "g0", "s1", "g1", "g2", "t3", "go", "s2", "b1", "b2", "t4", "s3", "t5", "s4", "w", "u", "s5", "s6", "t6", "p"),
 )
 
@@ -639,7 +639,7 @@
         ],
         compiler_params=pltpu.CompilerParams(collective_id=0, has_side_effects=True, vmem_limit_bytes=VMEM_LIMIT),
         name="iterations",
-    )(positions, obj, probe, amps, right, left, jnp.asarray(sorting()))
+    )(jnp.swapaxes(positions, 2, 3), obj, probe, amps, right, left, jnp.asarray(sorting()))
 
 
 def solution(mesh):

time: 127 us -> 124 us (0.976)
  Pallas kernels: 122 us -> 120 us
  local copies, waits for them, and re-layouts: 4.07 us -> 2.72 us
    pallas_call x1, Pallas kernels: 122 us -> 120 us  [shards(): pl.pallas_call(kernel, out_shape=(tile, tile), in_specs=[SMEM] + [VMEM] *...]
    unnamed x5 -> x4, local copies, waits for them, and re-layouts: 4.07 us -> 2.72 us
where the time goes in v6:
time: 124 us
  Pallas kernels  120 us (97%)
  local copies, waits for them, and re-layouts  2.72 us (2%)
    pallas_call x1, Pallas kernels, shards(): pl.pallas_call(kernel, out_shape=(tile, tile), in_specs=[SMEM] + [VMEM] *...  120 us
    unnamed x4, local copies, waits for them, and re-layouts  2.72 us

profile of v6, /device:TPU:1, one launch (start us, length us, event | category | flops | bytes accessed | tf_op | source)
XLA Modules:
  0.0 123.5 jit_solution(2075564225305276488)
XLA Ops:
  0.6 120.1 %iterations.1 = (f32[2,256,256]{2,1,0:T(8,128)}, f32[2,256,256]{2,1,0:T(8,128)}) custom-call(s32[1,1,2,8]{3,2,1,0:T(2,128)} %bitcast.1, f32[2,256,256]{2,1,0:T(8,128)} %obj.1, f32[2,256,256]{2,1,0:T(8,128)} %probe.1, bf16[1,1,8,256,256]{4,3,2,1,0:T(8,128)(2,1)} %amps_far.1, bf16[2,2,256,256]{3,2,1,0:T(8,128)(2,1)} %constant.6.clone.right_far, ...), custom_call_target="tpu_custom_call" | custom-call | tf_op jit(solution)/shard_map/iterations/pallas_call | solution.py:611
  120.8 0.0 copy-start
  120.8 1.9 %copy.11 = f32[2,256,256]{2,1,0:T(8,128)} copy(f32[2,256,256]{2,1,0:T(8,128)} %get-tuple-element.4) | data formatting | bytes 1048576
  122.7 0.0 copy-done
  122.7 0.8 copy.12
Async XLA Ops:
  120.8 1.9 %copy-start = (f32[2,256,256]{2,1,0:T(8,128)S(1)}, f32[2,256,256]{2,1,0:T(8,128)}, u32[]{:S(2)}) copy-start(f32[2,256,256]{2,1,0:T(8,128)} %get-tuple-element.5) | copy-start | bytes 1572868

commit v7 on v6

--- a/solution.py
+++ b/solution.py
@@ -188,11 +188,9 @@
 
 
 def right_dot(hi, lo, m):
-    return jnp.dot(
-        jnp.concatenate([hi, lo, hi], axis=1),
-        jnp.concatenate([m[0], m[0], m[1]], axis=0),
-        preferred_element_type=F32,
-    )
+    rows = hi.shape[0]
+    first = jnp.dot(jnp.concatenate([hi, lo], axis=0), m[0], preferred_element_type=F32)
+    return first[:rows] + (first[rows:] + jnp.dot(hi, m[1], preferred_element_type=F32))
 
 
 def left_dot(m, hi, lo):

time: 124 us -> 124 us (level)
  no operation moved by 1% of the time
where the time goes in v7:
time: 124 us; the launch traced here: 123 us
  Pallas kernels  120 us (97%)
  local copies, waits for them, and re-layouts  2.72 us (2%)
    pallas_call x1, Pallas kernels, shards(): pl.pallas_call(kernel, out_shape=(tile, tile), in_specs=[SMEM] + [VMEM] *...  120 us
    unnamed x4, local copies, waits for them, and re-layouts  2.72 us

profile of v7, /device:TPU:1, one launch (start us, length us, event | category | flops | bytes accessed | tf_op | source)
XLA Modules:
  0.0 123.4 jit_solution(9416675816306145121)
XLA Ops:
  0.6 120.0 %iterations.1 = (f32[2,256,256]{2,1,0:T(8,128)}, f32[2,256,256]{2,1,0:T(8,128)}) custom-call(s32[1,1,2,8]{3,2,1,0:T(2,128)} %bitcast.1, f32[2,256,256]{2,1,0:T(8,128)} %obj.1, f32[2,256,256]{2,1,0:T(8,128)} %probe.1, bf16[1,1,8,256,256]{4,3,2,1,0:T(8,128)(2,1)} %amps_far.1, bf16[2,2,256,256]{3,2,1,0:T(8,128)(2,1)} %constant.6.clone.right_far, ...), custom_call_target="tpu_custom_call" | custom-call | tf_op jit(solution)/shard_map/iterations/pallas_call | solution.py:609
  120.7 0.0 copy-start
  120.7 1.9 %copy.11 = f32[2,256,256]{2,1,0:T(8,128)} copy(f32[2,256,256]{2,1,0:T(8,128)} %get-tuple-element.4) | data formatting | bytes 1048576
  122.6 0.0 copy-done
  122.6 0.8 copy.12
Async XLA Ops:
  120.7 1.9 %copy-start = (f32[2,256,256]{2,1,0:T(8,128)S(1)}, f32[2,256,256]{2,1,0:T(8,128)}, u32[]{:S(2)}) copy-start(f32[2,256,256]{2,1,0:T(8,128)} %get-tuple-element.5) | copy-start | bytes 1572868
